TPU v7x, 256 devices: a whole 4x4x8 slice. The times are simulated.
256 devices in a mesh: graph: 32 (over z, x), fsdp: 4 (over y), replica: 2 (over core).
Axes of the slice: x: 4, y: 4, z: 8, core: 2. Of those that a mesh axis runs over, the one named last changes fastest.
Arguments:
- states: bfloat16 [16384, 512], P('graph'), may hold values from -6 to 6
- weights: bfloat16 [5, 512, 512], P(None, 'fsdp'), may hold values from -0.25 to 0.25
- edge_tiles: bfloat16 [32, 4, 2, 48, 128, 128], P('graph', 'fsdp', 'replica'), may hold values from 0 to 0.26516504, as said below
- edge_owner: int32 [32, 4, 2, 48], P(None, 'fsdp', 'replica'), may hold values from 0 to 31, as said below
- edge_source: int32 [32, 4, 2, 48], P(None, 'fsdp', 'replica'), may hold values from 0 to 3
- edge_target: int32 [32, 4, 2, 48], P(None, 'fsdp', 'replica'), may hold values from 0 to 3
- edge_relation: int32 [32, 4, 2, 48], P(None, 'fsdp', 'replica'), may hold values from 0 to 3
- edge_count: int32 [32, 4, 2], P(None, 'fsdp', 'replica'), may hold values from 36 to 48, as said below
- cotangent: bfloat16 [16384, 512], P('graph'), may hold values from -6 to 6
Outputs:
- layer_output: float32 [16384, 512], P(('graph', 'fsdp', 'replica'))
- grad_states: float32 [16384, 512], P(('graph', 'fsdp', 'replica'))
- grad_weights: float32 [5, 512, 512], P(None, ('fsdp', 'replica'))
Inputs may be any that keep to these rules, and one draw needn't show every extreme that they name: `edge_owner`: among the live slots of one device at most 2 name the same owner group; the device with all 48 slots live names some owner group exactly 2 times. `edge_count`: live slots come first in each device's list; some device has all 48 live. `edge_tiles`: nonnegative edge weights; about a quarter of each tile's entries are nonzero.
All inputs are finite; a program needn't handle non-finite values.
Results may differ from a plain program's by a relative error of at most 0.0085.
Values may be sent and summed in bfloat16 or wider, within the bound.
A program may use at most 128 MiB of HBM per device.

v0:
```python
import jax
import jax.numpy as jnp
from jax import lax
from jax.sharding import PartitionSpec as P


def silu_slope(pre):
    sigma = jax.nn.sigmoid(pre)
    return sigma * (1.0 + pre * (1.0 - sigma))


def relation_apply(blocks, relation, rel_weights):
    count_blocks = blocks.shape[0]
    tile_side = blocks.shape[1]
    features = blocks.shape[2]
    grouped = blocks.reshape(count_blocks // 8, 8, tile_side, features)
    chosen_all = relation.reshape(count_blocks // 8, 8)

    def apply_group(packed):
        inputs, chosen = packed
        panels = jnp.take(rel_weights, chosen, axis=0)
        return jnp.einsum(
            "bnd,bde->bne", inputs, panels, preferred_element_type=jnp.float32
        ).astype(jnp.bfloat16)

    return lax.map(apply_group, (grouped, chosen_all)).reshape(count_blocks, tile_side, features)


def shards(
    states,
    weights,
    edge_tiles,
    edge_owner,
    edge_source,
    edge_target,
    edge_relation,
    edge_count,
    cotangent,
):
    groups = lax.axis_size("graph")
    myself = lax.axis_index("graph")
    shares = lax.axis_size(("fsdp", "replica"))
    my_share = lax.axis_index(("fsdp", "replica"))
    tile_side = edge_tiles.shape[-1]
    features = states.shape[1]
    local_rows = states.shape[0]
    blocks_here = local_rows // tile_side
    relations = weights.shape[0] - 1
    per_device = edge_owner.shape[-1]
    capacity = max(2, per_device // groups)
    share_rows = local_rows // shares
    full_weights = lax.all_gather(weights, "fsdp", axis=1, tiled=True)
    rel_weights = full_weights[:relations]
    self_weight = full_weights[relations]
    owners = edge_owner.reshape(groups, per_device)
    sources = edge_source.reshape(groups, per_device)
    targets = edge_target.reshape(groups, per_device)
    labels = edge_relation.reshape(groups, per_device)
    counts = edge_count.reshape(groups)
    positions = jnp.arange(per_device, dtype=jnp.int32)
    active = positions[None, :] < counts[:, None]
    earlier = (
        (owners[:, :, None] == owners[:, None, :])
        & active[:, :, None]
        & (positions[:, None] < positions[None, :])[None]
    )
    slot_rank = jnp.sum(earlier.astype(jnp.int32), axis=1)
    own_owner = owners[myself]
    own_active = active[myself]
    own_target = targets[myself]
    own_label = labels[myself]
    own_slot = own_owner * capacity + slot_rank[myself]
    slot_ids = jnp.arange(capacity, dtype=jnp.int32)
    matches = (
        active[:, None, :]
        & (owners == myself)[:, None, :]
        & (slot_rank[:, None, :] == slot_ids[None, :, None])
    )
    filled = jnp.any(matches, axis=2)
    slot_block = jnp.sum(jnp.where(matches, sources[:, None, :], 0), axis=2)
    slot_label = jnp.sum(jnp.where(matches, labels[:, None, :], 0), axis=2)
    state_blocks = states.reshape(blocks_here, tile_side, features)
    outgoing = jnp.take(state_blocks, slot_block.reshape(-1), axis=0).reshape(
        groups, capacity, tile_side, features
    )
    outgoing = jnp.where(filled[:, :, None, None], outgoing, jnp.zeros((), jnp.bfloat16))
    arrived = lax.all_to_all(outgoing, "graph", split_axis=0, concat_axis=0, tiled=True)
    fetched = jnp.take(
        arrived.reshape(groups * capacity, tile_side, features),
        jnp.where(own_active, own_slot, 0),
        axis=0,
    )
    transformed = relation_apply(fetched, own_label, rel_weights)
    tile_blocks = edge_tiles.reshape(per_device, tile_side, tile_side)
    landing = (
        own_target[None, :] == jnp.arange(blocks_here, dtype=jnp.int32)[:, None]
    ) & own_active[None, :]
    spread = jnp.where(landing[:, :, None, None], tile_blocks[None], jnp.zeros((), jnp.bfloat16))
    messages = jnp.einsum(
        "tenm,emd->tnd", spread, transformed, preferred_element_type=jnp.float32
    ).reshape(local_rows, features)
    own_states = lax.dynamic_slice_in_dim(states, my_share * share_rows, share_rows, 0)
    message_total = lax.psum(messages, ("fsdp", "replica"))
    pre_all = message_total + jnp.dot(states, self_weight, preferred_element_type=jnp.float32)
    slope_all = (cotangent.astype(jnp.float32) * silu_slope(pre_all)).astype(jnp.bfloat16)
    pre_own = lax.dynamic_slice_in_dim(pre_all, my_share * share_rows, share_rows, 0)
    slope_own = lax.dynamic_slice_in_dim(slope_all, my_share * share_rows, share_rows, 0)
    layer_output = jax.nn.silu(pre_own)
    slope_blocks = slope_all.reshape(blocks_here, tile_side, features)
    upstream = jnp.take(slope_blocks, own_target, axis=0)
    pulled = jnp.einsum(
        "enm,end->emd", tile_blocks, upstream, preferred_element_type=jnp.float32
    ).astype(jnp.bfloat16)
    pulled = jnp.where(own_active[:, None, None], pulled, jnp.zeros((), jnp.bfloat16))
    slot_all = jnp.arange(groups * capacity, dtype=jnp.int32)
    placing = ((own_slot[None, :] == slot_all[:, None]) & own_active[None, :]).astype(jnp.bfloat16)
    returned = jnp.einsum(
        "se,emd->smd", placing, pulled, preferred_element_type=jnp.float32
    ).astype(jnp.bfloat16)
    returned = returned.reshape(groups, capacity, tile_side, features)
    received = lax.all_to_all(returned, "graph", split_axis=0, concat_axis=0, tiled=True)
    pair_ids = jnp.arange(blocks_here * relations, dtype=jnp.int32)
    slot_pairs = (slot_block * relations + slot_label).reshape(-1)
    gathering = ((slot_pairs[None, :] == pair_ids[:, None]) & filled.reshape(-1)[None, :]).astype(
        jnp.bfloat16
    )
    pair_sums = jnp.einsum(
        "ps,smd->pmd",
        gathering,
        received.reshape(groups * capacity, tile_side, features),
        preferred_element_type=jnp.float32,
    ).astype(jnp.bfloat16)
    pair_sums = pair_sums.reshape(blocks_here, relations, tile_side, features)
    weight_grad = jnp.einsum(
        "bnd,brne->rde", state_blocks, pair_sums, preferred_element_type=jnp.float32
    )
    self_grad = jnp.dot(own_states.T, slope_own, preferred_element_type=jnp.float32)
    weight_terms = jnp.concatenate([weight_grad, self_grad[None]], axis=0)
    state_terms = jnp.einsum(
        "brne,rde->bnd", pair_sums, rel_weights, preferred_element_type=jnp.float32
    )
    state_terms = state_terms.reshape(local_rows, features)
    state_share, weight_share = (
        lax.psum_scatter(state_terms, ("fsdp", "replica"), scatter_dimension=0, tiled=True),
        lax.psum_scatter(weight_terms, ("fsdp", "replica"), scatter_dimension=1, tiled=True),
    )
    weight_total = lax.psum(weight_share, "graph")
    grad_states = state_share + jnp.dot(
        slope_own, self_weight.T, preferred_element_type=jnp.float32
    )
    return (layer_output, grad_states, weight_total)


def solution(mesh):
    return jax.shard_map(
        shards,
        mesh=mesh,
        in_specs=(
            P("graph", None),
            P(None, "fsdp", None),
            P("graph", "fsdp", "replica", None, None, None),
            P(None, "fsdp", "replica", None),
            P(None, "fsdp", "replica", None),
            P(None, "fsdp", "replica", None),
            P(None, "fsdp", "replica", None),
            P(None, "fsdp", "replica"),
            P("graph", None),
        ),
        out_specs=(
            P(("graph", "fsdp", "replica"), None),
            P(("graph", "fsdp", "replica"), None),
            P(None, ("fsdp", "replica"), None),
        ),
        check_vma=False,
    )
```

profile of v0, /device:TPU:24, one launch (start us, length us, event | category | flops | bytes accessed | tf_op | source)
XLA Modules:
  0.0 924.8 jit_solution(18431171564100548588)
XLA Ops:
  7.2 0.8 compare_and_fusion.1
  8.1 1.3 convert_reduce_fusion
  9.4 0.9 select_reduce_fusion
  10.4 0.1 fusion.30
  10.5 0.1 reshape.355
  10.6 0.1 copy.38
  10.7 0.1 copy.37
  10.9 5.4 gather_fusion.1
  16.3 7.6 select_select_fusion
  23.9 11.6 %all-to-all-start = ((bf16[32,2,128,512]{3,2,1,0:T(8,128)(2,1)}), bf16[32,2,128,512]{3,2,1,0:T(8,128)(2,1)}, u32[]{:S(2)}, u32[]{:S(2)}) async-start(bf16[32,2,128,512]{3,2,1,0:T(8,128)(2,1)} %select_select_fusion), calls=%async_computation | async-start | bytes 16777216 | tf_op jit(solution)/shard_map/all_to_all | solution.py:87
  35.5 0.7 all-gather.2.cloned.1.call-update
  36.2 0.2 all-reduce.3.cloned.1.call-start
  36.5 0.7 fusion.45
  37.1 0.7 fusion.48
  38.0 0.7 fusion.53
  38.8 0.7 fusion.49
  39.5 0.7 compare_and_fusion.3
  40.3 3.1 broadcast_select_fusion.1
  43.4 31.7 %all-gather.2.cloned.1.call-done = bf16[5,512,512]{2,1,0:T(8,128)(2,1)} async-done(((bf16[5,128,512]{2,1,0:T(8,128)(2,1)}), bf16[5,512,512]{2,1,0:T(8,128)(2,1)}) %all-gather.2.cloned.1.call-update) | async-done | bytes 2621456 | tf_op jit(solution)/shard_map/all_gather | solution.py:52
  75.1 148.8 %all-to-all-done = bf16[32,2,128,512]{3,2,1,0:T(8,128)(2,1)} async-done(((bf16[32,2,128,512]{3,2,1,0:T(8,128)(2,1)}), bf16[32,2,128,512]{3,2,1,0:T(8,128)(2,1)}, u32[]{:S(2)}, u32[]{:S(2)}) %all-to-all-start) | async-done | bytes 8388640 | tf_op jit(solution)/shard_map/all_to_all | solution.py:87
  223.9 8.4 gather_fusion.2
  232.3 6.3 broadcast_select_fusion
  238.5 44.2 %while.10 = (s32[]{:T(128)}, bf16[6,8,128,512]{3,2,1,0:T(8,128)(2,1)}, bf16[6,8,128,512]{3,2,1,0:T(8,128)(2,1)}, s32[6,8]{1,0:T(8,128)S(1)}, bf16[4,512,512]{2,1,0:T(8,128)(2,1)S(1)}, /*index=5*/s32[]{:T(128)}) while((s32[]{:T(128)}, bf16[6,8,128,512]{3,2,1,0:T(8,128)(2,1)}, bf16[6,8,128,512]{3,2,1,0:T(8,128)(2,1)}, s32[6,8]{1,0:T(8,128)S(1)}, ...), condition=%wide.region_4.5_spmd, body=%wide.region_3.4_spmd.sunk | while | flops 539493440 | bytes 14685437 | solution.py:26
  238.6 2.9 gather_fusion
  241.4 4.5 fusion.72
  245.9 2.8 gather_fusion
  248.8 4.5 fusion.72
  253.3 2.8 gather_fusion
  256.1 4.6 fusion.72
  260.7 2.8 gather_fusion
  263.6 4.5 fusion.72
  268.1 2.8 gather_fusion
  270.9 4.5 fusion.72
  275.4 2.8 gather_fusion
  278.3 4.5 fusion.72
  282.7 7.6 convolution_bitcast_fusion.3
  290.3 0.7 fusion.47
  291.0 70.4 %all-reduce.3.cloned.1.call-done = f32[512,512]{1,0:T(8,128)} async-done(((f32[512,512]{1,0:T(8,128)}), f32[512,512]{1,0:T(8,128)}) %all-reduce.3.cloned.1.call-update) | async-done | bytes 1048592 | tf_op jit(solution)/shard_map/psum | solution.py:103
  361.4 3.2 multiply_convert_fusion
  364.6 5.9 gather_fusion.3
  370.5 8.4 select_bitcast_fusion
  378.9 9.1 copy.43
  388.0 8.5 convolution_convert_fusion
  396.5 13.1 %reshape.359 = bf16[32,2,128,512]{3,1,0,2:T(2,128)(2,1)} reshape(bf16[64,128,512]{2,0,1:T(8,128)(2,1)} %convolution_convert_fusion) | data formatting | bytes 16777216 | tf_op jit(solution)/shard_map/reshape | solution.py:120
  409.6 8.1 copy.44
  417.7 9.9 %all-to-all-start.1 = ((bf16[32,2,128,512]{3,1,2,0:T(2,128)(2,1)}), bf16[32,2,128,512]{3,1,2,0:T(2,128)(2,1)}, u32[]{:S(2)}, u32[]{:S(2)}) async-start(bf16[32,2,128,512]{3,1,2,0:T(2,128)(2,1)} %copy.44), calls=%async_computation.1 | async-start | bytes 16777216 | tf_op jit(solution)/shard_map/all_to_all | solution.py:121
  427.7 0.1 and.112
  428.0 2.2 convolution_bitcast_fusion.1
  430.2 189.8 %all-to-all-done.1 = bf16[32,2,128,512]{3,1,2,0:T(2,128)(2,1)} async-done(((bf16[32,2,128,512]{3,1,2,0:T(2,128)(2,1)}), bf16[32,2,128,512]{3,1,2,0:T(2,128)(2,1)}, u32[]{:S(2)}, u32[]{:S(2)}) %all-to-all-start.1) | async-done | bytes 8388640 | tf_op jit(solution)/shard_map/all_to_all | solution.py:121
  620.0 8.1 copy.45
  628.1 13.1 %reshape.360 = bf16[64,128,512]{2,0,1:T(8,128)(2,1)} reshape(bf16[32,2,128,512]{3,1,0,2:T(2,128)(2,1)} %copy.45) | data formatting | bytes 16777216 | tf_op jit(solution)/shard_map/reshape | solution.py:130
  641.2 6.0 convolution_convert_fusion.1
  647.2 4.0 reshape.361
  651.1 4.8 convolution_bitcast_fusion
  656.0 3.0 pad_maximum_fusion
  659.0 9.2 copy.49
  668.2 2.8 copy.46
  670.9 2.3 convolution_bitcast_fusion.2
  673.3 52.6 %reduce-scatter.5.cloned.1.call-done = f32[5,64,512]{2,0,1:T(8,128)} async-done(((f32[5,512,512]{2,0,1:T(8,128)}), f32[5,64,512]{2,0,1:T(8,128)}) %reduce-scatter.5.cloned.1.call-update) | async-done | bytes 655376 | tf_op jit(solution)/shard_map/reduce_scatter | solution.py:145
  725.9 1.6 divide_multiply_fusion
  727.5 33.6 %reduce-scatter.3.cloned.1.call-done = f32[64,512]{1,0:T(8,128)} async-done(((f32[512,512]{1,0:T(8,128)}), f32[64,512]{1,0:T(8,128)}) %reduce-scatter.3.cloned.1.call-update) | async-done | bytes 131088 | tf_op jit(solution)/shard_map/reduce_scatter | solution.py:144
  761.2 1.9 convolution_add_fusion.1
  763.0 152.8 %all-reduce.5.cloned.1.call-done = f32[5,64,512]{2,0,1:T(8,128)} async-done(((f32[5,64,512]{2,0,1:T(8,128)}), f32[5,64,512]{2,0,1:T(8,128)}) %all-reduce.5.cloned.1.call-update) | async-done | bytes 655376 | tf_op jit(solution)/shard_map/psum | solution.py:147
  915.9 2.4 copy.50
  (54 shorter events, 1.2 us)
Async XLA Ops:
  7.2 3.7 copy-start
  23.9 16.4 %copy-start.3 = (bf16[1,1,1,48,128,128]{5,4,3,2,1,0:T(8,128)(2,1)S(1)}, bf16[1,1,1,48,128,128]{5,4,3,2,1,0:T(8,128)(2,1)}, u32[]{:S(2)}) copy-start(bf16[1,1,1,48,128,128]{5,4,3,2,1,0:T(8,128)(2,1)} %param.13) | copy-start | bytes 4718596
  23.9 200.0 %all-to-all-start = ((bf16[32,2,128,512]{3,2,1,0:T(8,128)(2,1)}), bf16[32,2,128,512]{3,2,1,0:T(8,128)(2,1)}, u32[]{:S(2)}, u32[]{:S(2)}) async-start(bf16[32,2,128,512]{3,2,1,0:T(8,128)(2,1)} %select_select_fusion), calls=%async_computation | async-start | bytes 16777216 | tf_op jit(solution)/shard_map/all_to_all | solution.py:87
  35.5 39.6 %all-gather.2.cloned.1.call-start = ((), (), s32[]{:S(2)}) async-start(), calls=%async_computation.4 | async-start | bytes 3276800 | tf_op jit(solution)/shard_map/all_gather | solution.py:52
  36.2 325.1 %all-reduce.3.cloned.1.call-start = ((), (), s32[]{:S(2)}) async-start(), calls=%async_computation.5 | async-start | bytes 2097152 | tf_op jit(solution)/shard_map/psum | solution.py:103
  232.3 6.3 slice-start
  282.7 78.6 %copy-start.1 = (bf16[5,512,512]{2,1,0:T(8,128)(2,1)S(1)}, bf16[5,512,512]{2,1,0:T(8,128)(2,1)}, u32[]{:S(2)}) copy-start(bf16[5,512,512]{2,1,0:T(8,128)(2,1)} %all-gather.2.cloned.1.call-done) | copy-start | bytes 7864324
  417.7 202.3 %all-to-all-start.1 = ((bf16[32,2,128,512]{3,1,2,0:T(2,128)(2,1)}), bf16[32,2,128,512]{3,1,2,0:T(2,128)(2,1)}, u32[]{:S(2)}, u32[]{:S(2)}) async-start(bf16[32,2,128,512]{3,1,2,0:T(2,128)(2,1)} %copy.44), calls=%async_computation.1 | async-start | bytes 16777216 | tf_op jit(solution)/shard_map/all_to_all | solution.py:121
  427.6 298.3 %reduce-scatter.5.cloned.1.call-start = ((), (), s32[]{:S(2)}) async-start(), calls=%async_computation.7 | async-start | bytes 9437184 | tf_op jit(solution)/shard_map/reduce_scatter | solution.py:145
  651.1 4.9 copy-start.2
  668.1 93.0 %reduce-scatter.3.cloned.1.call-start = ((), (), s32[]{:S(2)}) async-start(), calls=%async_computation.6 | async-start | bytes 1179648 | tf_op jit(solution)/shard_map/reduce_scatter | solution.py:144
  673.2 242.6 %all-reduce.5.cloned.1.call-start = ((), (), s32[]{:S(2)}) async-start(), calls=%async_computation.8 | async-start | bytes 2097152 | tf_op jit(solution)/shard_map/psum | solution.py:147
Sparse Core Ops, SparseCore 0:
  38.1 36.9 all-gather.1
  290.4 70.8 all-reduce.2
  668.3 57.5 reduce-scatter.4
  728.3 32.8 reduce-scatter.2
  764.5 151.3 all-reduce.4
where the time goes:
time: 927 us; the launch traced here: 925 us
  waiting for transfers between devices  680 us (73%)
  local copies, waits for them, and re-layouts  108 us (12%)
  matrix products  71.7 us (8%)
  other arithmetic  28.4 us (3%)
  starting transfers between devices  21.9 us (2%)
  between operations  13.9 us (1%)
    all_to_all x1, waiting for transfers between devices, shards(): lax.all_to_all(returned, 'graph', split_axis=0, concat_axis=0, tiled=True)  190 us
    psum x1, waiting for transfers between devices, shards(): weight_total = lax.psum(weight_share, 'graph')  153 us
    all_to_all x1, waiting for transfers between devices, shards(): lax.all_to_all(outgoing, 'graph', split_axis=0, concat_axis=0, tiled=True)  149 us
    psum x1, waiting for transfers between devices, shards(): message_total = lax.psum(messages, ('fsdp', 'replica'))  70.4 us
    reduce_scatter x1, waiting for transfers between devices, shards(): lax.psum_scatter(weight_terms, ('fsdp', 'replica'), scatter_dimension=1,...  52.6 us
    reduce_scatter x1, waiting for transfers between devices, shards(): lax.psum_scatter(state_terms, ('fsdp', 'replica'), scatter_dimension=0, t...  33.6 us
    all_gather x1, waiting for transfers between devices, shards(): full_weights = lax.all_gather(weights, 'fsdp', axis=1, tiled=True)  31.7 us
    dot_general x6, matrix products, apply_group(): jnp.einsum('bnd,bde->bne', inputs, panels, preferred_element_type=jnp.flo...  26.9 us
  transfers between devices with their start and end apart: 7, of which 7 were waited for; matrix products, arithmetic and copies ran while one was open for 2% of the time, Pallas kernels for 0%

commit v1 on v0

v1 whole, which is shorter than its diff:
```python
import jax
import jax.numpy as jnp
from jax import lax
from jax.experimental import pallas as pl
from jax.experimental.pallas import tpu as pltpu
from jax.sharding import PartitionSpec as P

D = 512
REL = 4
TILE = 128
EB = 48
NZ = 8
NX = 4
NY = 4
NC = 8
SLOTS = 8
ROWS = 64
WR = 160
WC = 128
BF = jnp.bfloat16
F32 = jnp.float32
MESH = pl.DeviceIdType.MESH
ANY = pl.BlockSpec(memory_space=pl.ANY)
VM = pl.BlockSpec(memory_space=pltpu.VMEM)
SM = pl.BlockSpec(memory_space=pltpu.SMEM)
DMA = pltpu.SemaphoreType.DMA


def params(collective=None):
    more = {} if collective is None else {"collective_id": collective, "has_side_effects": True}
    return pltpu.CompilerParams(vmem_limit_bytes=56 * 1024 * 1024, **more)


def place():
    g = lax.axis_index("graph")
    return g // NX, g % NX, lax.axis_index("fsdp"), lax.axis_index("replica")


def send(src, dst, ssem, rsem, z, x, y, p):
    return pltpu.make_async_remote_copy(
        src_ref=src,
        dst_ref=dst,
        send_sem=ssem,
        recv_sem=rsem,
        device_id=(z * NX + x, y, p),
        device_id_type=MESH,
    )


def greet(partners, swap=None):
    barrier = pltpu.get_barrier_semaphore()
    for z, x, y, p in partners:
        pl.semaphore_signal(barrier, inc=1, device_id=(z * NX + x, y, p), device_id_type=MESH)
    if swap is not None:
        (z, x, y, p), is_self = swap

        @pl.when(jnp.logical_not(is_self))
        def _():
            pl.semaphore_signal(barrier, inc=1, device_id=(z * NX + x, y, p), device_id_type=MESH)

        pl.semaphore_wait(barrier, len(partners) + jnp.where(is_self, 0, 1))
    else:
        pl.semaphore_wait(barrier, len(partners))


def group_peers(z, x, y, p):
    return [
        (z, x, (y + dy) % NY, (p + dp) % 2)
        for dy, dp in ((0, 1), (1, 0), (3, 0), (1, 1), (3, 1), (2, 0), (2, 1))
    ]


def x_peers(z, x, y, p):
    return [(z, (x + i) % NX, y, p) for i in (1, 2, 3)]


def z_peers(z, x, y, p, steps=(1, 7)):
    return [((z + i) % NZ, x, y, p) for i in steps]


def swap_of(z, x, y, p):
    return (2 * (z // 2) + p, y, x, z % 2), (x == y) & (z % 2 == p)


def pack_kernel(owner, source, target, relation, count, tiles, packed, meta, filled):
    g = lax.axis_index("graph")
    for c in range(NC):
        for s in range(SLOTS):
            meta[c, 0, s] = -1

    def clear(o, carry):
        filled[o] = 0
        return carry

    lax.fori_loop(0, NZ * NX, clear, 0)

    def put(e, carry):
        o = owner[g, e]
        rank = filled[o]
        filled[o] = rank + 1
        c = (o % NX) * 2 + (o // NX) % 2
        s = (o // 8) * 2 + rank
        meta[c, 0, s] = source[g, e] + 4 * target[g, e] + 16 * relation[g, e]
        packed[c, s] = tiles[e]
        return carry

    lax.fori_loop(0, count[g], put, 0)


def pack(owner, source, target, relation, count, tiles):
    return pl.pallas_call(
        pack_kernel,
        out_shape=(
            jax.ShapeDtypeStruct((NC, SLOTS, TILE, TILE), BF),
            jax.ShapeDtypeStruct((NC, 8, 128), jnp.int32),
        ),
        in_specs=[SM] * 5 + [VM],
        out_specs=(VM, SM),
        scratch_shapes=[pltpu.SMEM((NZ * NX,), jnp.int32)],
        compiler_params=params(),
    )(owner, source, target, relation, count, tiles)


def deal_kernel(
    packed, meta, states, tiles_o, meta_o, xp,
    own_sems, t_send, t_recv, m_send, m_recv, v_send, v_recv, x_send, x_recv, z_send, z_recv,
):
    z, x, y, p = place()
    peers = group_peers(z, x, y, p)
    xs = x_peers(z, x, y, p)
    up, down = z_peers(z, x, y, p)
    target, is_self = swap_of(z, x, y, p)
    greet(peers + xs + [up, down], (target, is_self))
    c = y * 2 + p
    piece = states.at[pl.ds(pl.multiple_of((p * NY + y) * ROWS, ROWS), ROWS)]

    @pl.when(jnp.logical_not(is_self))
    def _():
        send(piece, xp.at[target[0], target[1]], v_send, v_recv, *target).start()

    @pl.when(is_self)
    def _():
        pltpu.make_async_copy(piece, xp.at[z, x], own_sems.at[0]).start()

    mine = pltpu.make_async_copy(packed.at[c], tiles_o.at[c], own_sems.at[1])
    mine_meta = pltpu.make_async_copy(meta.at[c], meta_o.at[c], own_sems.at[2])
    mine.start()
    mine_meta.start()
    tile_copies = []
    for i, q in enumerate(peers):
        cq = q[2] * 2 + q[3]
        a = send(packed.at[cq], tiles_o.at[c], t_send.at[i], t_recv.at[i], *q)
        b = send(meta.at[cq], meta_o.at[c], m_send.at[i], m_recv.at[i], *q)
        a.start()
        b.start()
        tile_copies += [a, b]

    @pl.when(jnp.logical_not(is_self))
    def _():
        send(piece, xp.at[z, x], v_send, v_recv, *target).wait()

    @pl.when(is_self)
    def _():
        pltpu.make_async_copy(piece, xp.at[z, x], own_sems.at[0]).wait()

    x_copies = [
        send(xp.at[z, x], xp.at[z, x], x_send.at[i], x_recv.at[i], *q) for i, q in enumerate(xs)
    ]
    for a in x_copies:
        a.start()

    z_copies = {}
    for s in range(4):
        for i in range(NX):
            xi = (x + i) % NX
            if s == 0 and i > 0:
                x_copies[3 - i].wait_recv()
            for d, q in ((0, up), (1, down)):
                if s > 0 and (d, s - 1, i) in z_copies:
                    z_copies[d, s - 1, i].wait_recv()
                if s < 3 or (i < 2) == (d == 0):
                    zs = (z - s + NZ) % NZ if d == 0 else (z + s) % NZ
                    a = send(xp.at[zs, xi], xp.at[zs, xi], z_send.at[d, s, i], z_recv.at[d, s, i], *q)
                    a.start()
                    z_copies[d, s, i] = a
    for (d, s, i), a in z_copies.items():
        if s == 3:
            a.wait_recv()
    for a in x_copies + list(z_copies.values()):
        a.wait_send()
    mine.wait()
    mine_meta.wait()
    for a in tile_copies:
        a.wait()


def deal(packed, meta, states):
    return pl.pallas_call(
        deal_kernel,
        out_shape=(
            jax.ShapeDtypeStruct((NC, SLOTS, TILE, TILE), BF),
            jax.ShapeDtypeStruct((NC, 8, 128), jnp.int32),
            jax.ShapeDtypeStruct((NZ, NX, ROWS, D), BF),
        ),
        in_specs=[ANY] * 3,
        out_specs=(ANY, ANY, ANY),
        scratch_shapes=[
            DMA((3,)), DMA((7,)), DMA((7,)), DMA((7,)), DMA((7,)), DMA(()), DMA(()),
            DMA((3,)), DMA((3,)), DMA((2, 4, 4)), DMA((2, 4, 4)),
        ],
        compiler_params=params(0),
    )(packed, meta, states)


def forward_kernel(meta, tiles, xp, weights, t_out, m_out, acc):
    acc[...] = jnp.zeros_like(acc)

    def slot(i, carry):
        c = i // SLOTS
        s = i % SLOTS
        code = meta[c, 0, s]

        @pl.when(code >= 0)
        def _():
            source = pl.multiple_of(((s // 2) * 4 + code % 4) * TILE, TILE)
            into = pl.multiple_of((code // 4) * TILE, TILE)
            got = jnp.dot(tiles[c, s], xp[pl.ds(source, TILE), :], preferred_element_type=F32)
            acc[pl.ds(into, TILE), :] += got

        return carry

    lax.fori_loop(0, NC * SLOTS, slot, 0)
    total = jnp.zeros((D, D), F32)
    for r in range(REL):
        t = acc[r * D : (r + 1) * D, :].astype(BF)
        t_out[r] = t
        total = total + jnp.dot(t, weights[r], preferred_element_type=F32)
    m_out[...] = total.astype(BF).reshape(m_out.shape)


def forward(meta, tiles, xp, weights):
    return pl.pallas_call(
        forward_kernel,
        out_shape=(
            jax.ShapeDtypeStruct((REL, D, D), BF),
            jax.ShapeDtypeStruct((NC, ROWS, D), BF),
        ),
        in_specs=[SM, VM, VM, VM],
        out_specs=(VM, VM),
        scratch_shapes=[pltpu.VMEM((REL * D, D), F32)],
        compiler_params=params(),
    )(meta, tiles, xp, weights)


def slope_kernel(
    m_in, x_own, cot_own, weights, out_o, slope_o, self_o, m_recv, mine, s1, r1, s2, r2, own_sem
):
    z, x, y, p = place()
    peers = group_peers(z, x, y, p)
    greet(peers)
    c = y * 2 + p
    first = []
    for i, q in enumerate(peers):
        a = send(m_in.at[q[2] * 2 + q[3]], m_recv.at[i], s1.at[i], r1.at[i], *q)
        a.start()
        first.append(a)
    w = weights[REL]
    pre = m_in[c].astype(F32) + jnp.dot(x_own[...], w, preferred_element_type=F32)
    for i, a in enumerate(first):
        a.wait_recv()
        pre = pre + m_recv[i].astype(F32)
    sigma = jax.nn.sigmoid(pre)
    slope = (cot_own[...].astype(F32) * (sigma * (1.0 + pre * (1.0 - sigma)))).astype(BF)
    mine[...] = slope
    second = []
    for i, q in enumerate(peers):
        a = send(mine, slope_o.at[c], s2.at[i], r2.at[i], *q)
        a.start()
        second.append(a)
    slope_o[c] = slope
    out_o[...] = pre * sigma
    self_o[...] = lax.dot_general(
        slope, w, (((1,), (1,)), ((), ())), preferred_element_type=F32
    )
    for a in first:
        a.wait_send()
    for a in second:
        a.wait()


def slopes(m_in, x_own, cot_own, weights):
    return pl.pallas_call(
        slope_kernel,
        out_shape=(
            jax.ShapeDtypeStruct((ROWS, D), F32),
            jax.ShapeDtypeStruct((NC, ROWS, D), BF),
            jax.ShapeDtypeStruct((ROWS, D), F32),
        ),
        in_specs=[VM] * 4,
        out_specs=(VM, VM, VM),
        scratch_shapes=[
            pltpu.VMEM((7, ROWS, D), BF), pltpu.VMEM((ROWS, D), BF),
            DMA((7,)), DMA((7,)), DMA((7,)), DMA((7,)), DMA(()),
        ],
        compiler_params=params(1),
    )(m_in, x_own, cot_own, weights)


def backward_kernel(meta, tiles, slope, weights, t_in, x_own, s_own, g_out, w_out, zs, acc):
    over_rows = (((0,), (0,)), ((), ()))
    over_columns = (((1,), (1,)), ((), ()))
    acc[...] = jnp.zeros_like(acc)
    for r in range(REL):
        zs[r * D : (r + 1) * D, :] = lax.dot_general(
            slope[...], weights[r], over_columns, preferred_element_type=F32
        ).astype(BF)

    def slot(i, carry):
        c = i // SLOTS
        s = i % SLOTS
        code = meta[c, 0, s]

        @pl.when(code >= 0)
        def _():
            into = pl.multiple_of(((s // 2) * 4 + code % 4) * TILE, TILE)
            source = pl.multiple_of((code // 4) * TILE, TILE)
            got = lax.dot_general(
                tiles[c, s], zs[pl.ds(source, TILE), :], over_rows, preferred_element_type=F32
            )
            acc[pl.ds(into, TILE), :] += got

        return carry

    lax.fori_loop(0, NC * SLOTS, slot, 0)
    for k in range(4):
        for b in range(4):
            for h in range(2):
                row = (k * 4 + b) * TILE + h * ROWS
                g_out[2 * k + h, b] = acc[row : row + ROWS, :].astype(BF)
    for m in range(REL + 1):
        if m < REL:
            part = lax.dot_general(t_in[m], slope[...], over_rows, preferred_element_type=F32)
        else:
            part = lax.dot_general(x_own[...], s_own[...], over_rows, preferred_element_type=F32)
        part = part.astype(BF)
        for c in range(NC):
            for q in range(4):
                for low, high in ((0, 32), (32, 64)):
                    row = m * ROWS + low
                    w_out[c, (row // WR) * 4 + q, row % WR : row % WR + 32, :] = part[
                        c * ROWS + low : c * ROWS + high, q * WC : (q + 1) * WC
                    ]


def backward(meta, tiles, slope, weights, t_in, x_own, s_own):
    return pl.pallas_call(
        backward_kernel,
        out_shape=(
            jax.ShapeDtypeStruct((NZ, NX, ROWS, D), BF),
            jax.ShapeDtypeStruct((NC, NZ, WR, WC), BF),
        ),
        in_specs=[SM] + [VM] * 6,
        out_specs=(VM, VM),
        scratch_shapes=[pltpu.VMEM((REL * D, D), BF), pltpu.VMEM((16 * TILE, D), F32)],
        compiler_params=params(),
    )(meta, tiles, slope, weights, t_in, x_own, s_own)


def reduce_kernel(
    g_in, w_in, self_in, g_out, w_out,
    c_buf, y_src, y_buf, y_own, zw_src, zw_buf, xw_src, xw_buf, aw_buf,
    g_src, g_buf, gx_src, gx_buf, v_src, v_buf,
    c_s, c_r, y_s, y_r, zw_s, zw_r, xw_s, xw_r, aw_s, aw_r, g_s, g_r, gx_s, gx_r, v_s, v_r,
):
    z, x, y, p = place()
    core = (z, x, y, 1 - p)
    ys = [(z, x, (y + i) % NY, p) for i in (1, 3, 2)]
    xs = x_peers(z, x, y, p)
    around = z_peers(z, x, y, p, (1, 7, 2, 6, 3, 5, 4))
    up, down = around[0], around[1]
    target, is_self = swap_of(z, x, y, p)
    greet([core] + ys + xs + around, (target, is_self))

    c_copies = []
    for i in range(NY):
        yi = (y + i) % NY
        a = send(w_in.at[yi * 2 + 1 - p], c_buf.at[yi], c_s.at[i], c_r.at[i], *core)
        a.start()
        c_copies.append(a)

    g_copies = {}
    hops = {(d, i): 4 if (i < 2) == (d == 0) else 3 for d in range(2) for i in range(NX)}

    def chain(s):
        for i in range(NX):
            xi = (x + i) % NX
            for d, q in ((0, up), (1, down)):
                left = hops[d, i] - s
                if left <= 0:
                    continue
                zd = (z + left) % NZ if d == 0 else (z - left + NZ) % NZ
                if s == 0:
                    src = g_in.at[zd, xi]
                else:
                    g_copies[d, s - 1, i].wait_recv()
                    g_src[d, s - 1, i] = (
                        g_in[zd, xi].astype(F32) + g_buf[d, s - 1, i].astype(F32)
                    ).astype(BF)
                    src = g_src.at[d, s - 1, i]
                a = send(src, g_buf.at[d, s, i], g_s.at[d, s, i], g_r.at[d, s, i], *q)
                a.start()
                g_copies[d, s, i] = a

    chain(0)
    y_copies = []
    for j, q in enumerate(ys):
        i = (1, 3, 2)[j]
        yi = q[2]
        c_copies[i].wait_recv()
        y_src[j] = (w_in[yi * 2 + p].astype(F32) + c_buf[yi].astype(F32)).astype(BF)
        a = send(y_src.at[j], y_buf.at[j], y_s.at[j], y_r.at[j], *q)
        a.start()
        y_copies.append(a)
    c_copies[0].wait_recv()
    y_own[...] = w_in[y * 2 + p].astype(F32) + c_buf[y].astype(F32)
    chain(1)
    chain(2)

    total = y_own[...]
    for j, a in enumerate(y_copies):
        a.wait_recv()
        total = total + y_buf[j].astype(F32)
    zw_src[...] = total.astype(BF)
    zw_copies = []
    for i, q in enumerate(around):
        a = send(zw_src.at[q[0]], zw_buf.at[i], zw_s.at[i], zw_r.at[i], *q)
        a.start()
        zw_copies.append(a)
    chain(3)

    gx_copies = []
    own = None
    for i in (1, 2, 3, 0):
        xi = (x + i) % NX
        part = g_in[z, xi].astype(F32)
        for d in range(2):
            last = hops[d, i] - 1
            g_copies[d, last, i].wait_recv()
            part = part + g_buf[d, last, i].astype(F32)
        if i:
            gx_src[i - 1] = part.astype(BF)
            a = send(gx_src.at[i - 1], gx_buf.at[i - 1], gx_s.at[i - 1], gx_r.at[i - 1], *xs[i - 1])
            a.start()
            gx_copies.append(a)
        else:
            own = part

    mine = zw_src[z].astype(F32)
    for i, a in enumerate(zw_copies):
        a.wait_recv()
        mine = mine + zw_buf[i].astype(F32)
    xw_src[...] = mine.astype(BF)
    xw_copies = []
    for i, q in enumerate(xs):
        a = send(xw_src, xw_buf.at[x], xw_s.at[i], xw_r.at[i], *q)
        a.start()
        xw_copies.append(a)
    xw_buf[x] = xw_src[...]

    for i, a in enumerate(gx_copies):
        a.wait_recv()
        own = own + gx_buf[i].astype(F32)
    v_src[...] = own.astype(BF)

    @pl.when(jnp.logical_not(is_self))
    def _():
        send(v_src, v_buf, v_s, v_r, *target).start()

    @pl.when(is_self)
    def _():
        v_buf[...] = v_src[...]

    for a in xw_copies:
        a.wait_recv()
    done = xw_buf[0].astype(F32)
    for i in range(1, NX):
        done = done + xw_buf[i].astype(F32)
    aw_buf[z] = done.astype(BF)
    aw_copies = []
    for i, q in enumerate(around):
        a = send(aw_buf.at[z], aw_buf.at[z], aw_s.at[i], aw_r.at[i], *q)
        a.start()
        aw_copies.append(a)

    @pl.when(jnp.logical_not(is_self))
    def _():
        send(v_src, v_buf, v_s, v_r, *target).wait()

    g_out[...] = v_buf[...].astype(F32) + self_in[...]
    for a in aw_copies:
        a.wait_recv()
    for m in range(REL + 1):
        for q in range(4):
            for low in (0, 32):
                row = m * ROWS + low
                w_out[m, low : low + 32, q * WC : (q + 1) * WC] = aw_buf[
                    (row // WR) * 4 + q, row % WR : row % WR + 32, :
                ].astype(F32)
    for a in c_copies + y_copies + zw_copies + xw_copies + aw_copies + gx_copies:
        a.wait_send()
    for a in g_copies.values():
        a.wait_send()


def reduce(g_in, w_in, self_in):
    return pl.pallas_call(
        reduce_kernel,
        out_shape=(
            jax.ShapeDtypeStruct((ROWS, D), F32),
            jax.ShapeDtypeStruct((REL + 1, ROWS, D), F32),
        ),
        in_specs=[VM] * 3,
        out_specs=(VM, VM),
        scratch_shapes=[
            pltpu.VMEM((NY, NZ, WR, WC), BF),
            pltpu.VMEM((3, NZ, WR, WC), BF),
            pltpu.VMEM((3, NZ, WR, WC), BF),
            pltpu.VMEM((NZ, WR, WC), F32),
            pltpu.VMEM((NZ, WR, WC), BF),
            pltpu.VMEM((7, WR, WC), BF),
            pltpu.VMEM((WR, WC), BF),
            pltpu.VMEM((NX, WR, WC), BF),
            pltpu.VMEM((NZ, WR, WC), BF),
            pltpu.VMEM((2, 3, NX, ROWS, D), BF),
            pltpu.VMEM((2, 4, NX, ROWS, D), BF),
            pltpu.VMEM((3, ROWS, D), BF),
            pltpu.VMEM((3, ROWS, D), BF),
            pltpu.VMEM((ROWS, D), BF),
            pltpu.VMEM((ROWS, D), BF),
            DMA((4,)), DMA((4,)), DMA((3,)), DMA((3,)), DMA((7,)), DMA((7,)), DMA((3,)), DMA((3,)),
            DMA((7,)), DMA((7,)), DMA((2, 4, 4)), DMA((2, 4, 4)), DMA((3,)), DMA((3,)), DMA(()), DMA(()),
        ],
        compiler_params=params(2),
    )(g_in, w_in, self_in)


def shards(
    states,
    weights,
    edge_tiles,
    edge_owner,
    edge_source,
    edge_target,
    edge_relation,
    edge_count,
    cotangent,
):
    groups = edge_owner.shape[0]
    share = lax.axis_index(("fsdp", "replica"))
    full = lax.all_gather(weights, "fsdp", axis=1, tiled=True)
    owner = edge_owner.reshape(groups, EB)
    source = edge_source.reshape(groups, EB)
    target = edge_target.reshape(groups, EB)
    relation = edge_relation.reshape(groups, EB)
    count = edge_count.reshape(groups)
    tiles = edge_tiles.reshape(EB, TILE, TILE)
    packed, meta = pack(owner, source, target, relation, count, tiles)
    tiles, meta, xp = deal(packed, meta, states)
    t_all, m_part = forward(meta, tiles, xp.reshape(-1, D), full)
    x_own = lax.dynamic_slice_in_dim(states, share * ROWS, ROWS, 0)
    cot_own = lax.dynamic_slice_in_dim(cotangent, share * ROWS, ROWS, 0)
    layer_output, slope, self_part = slopes(m_part, x_own, cot_own, full)
    s_own = lax.dynamic_slice_in_dim(slope, share, 1, 0).reshape(ROWS, D)
    g_part, w_part = backward(meta, tiles, slope.reshape(-1, D), full, t_all, x_own, s_own)
    grad_states, grad_weights = reduce(g_part, w_part, self_part)
    return layer_output, grad_states, grad_weights


def solution(mesh):
    return jax.shard_map(
        shards,
        mesh=mesh,
        in_specs=(
            P("graph", None),
            P(None, "fsdp", None),
            P("graph", "fsdp", "replica", None, None, None),
            P(None, "fsdp", "replica", None),
            P(None, "fsdp", "replica", None),
            P(None, "fsdp", "replica", None),
            P(None, "fsdp", "replica", None),
            P(None, "fsdp", "replica"),
            P("graph", None),
        ),
        out_specs=(
            P(("graph", "fsdp", "replica"), None),
            P(("graph", "fsdp", "replica"), None),
            P(None, ("fsdp", "replica"), None),
        ),
        check_vma=False,
    )
```

time: 927 us -> 192 us (0.21)
  waiting for transfers between devices: 680 us -> 5.54 us
  Pallas kernels: 0 us -> 162 us
  local copies, waits for them, and re-layouts: 108 us -> 7.23 us
  matrix products: 71.7 us -> 0 us
  other arithmetic: 28.4 us -> 0 us
  starting transfers between devices: 21.9 us -> 0.04 us
    all_to_all x2 -> x0, waiting for transfers between devices: 339 us -> none  [the longest x1 190 us: shards(): lax.all_to_all(returned, 'graph', split_axis=0, concat_axis=0, tiled=True)]
    psum x2 -> x0, waiting for transfers between devices: 223 us -> none  [the longest x1 153 us: shards(): weight_total = lax.psum(weight_share, 'graph')]
    pallas_call x0 -> x6, Pallas kernels: none -> 162 us  [the longest x1 57.7 us: reduce(): pl.pallas_call(reduce_kernel, out_shape=(jax.ShapeDtypeStruct((ROWS, D),...]
    reduce_scatter x2 -> x0, waiting for transfers between devices: 86.3 us -> none  [the longest x1 52.6 us: shards(): lax.psum_scatter(weight_terms, ('fsdp', 'replica'), scatter_dimension=1,...]
    dot_general x15 -> x0, matrix products: 71.7 us -> none  [the longest x6 26.9 us: apply_group(): jnp.einsum('bnd,bde->bne', inputs, panels, preferred_element_type=jnp.flo...]
    reshape x5 -> x1, local copies, waits for them, and re-layouts: 38.4 us -> 1.48 us  [shards(): s_own = lax.dynamic_slice_in_dim(slope, share, 1, 0).reshape(ROWS, D)]
    gather x9 -> x0, local copies, waits for them, and re-layouts: 36.8 us -> none  [the longest x6 17.1 us: apply_group(): panels = jnp.take(rel_weights, chosen, axis=0)]
    all_gather x1, waiting for transfers between devices: 31.7 us -> 4.86 us  [shards(): full = lax.all_gather(weights, 'fsdp', axis=1, tiled=True)]
  transfers between devices with their start and end apart: 7 -> 1, of which waited for: 7 -> 1; matrix products, arithmetic and copies ran while one was open for 2% -> 1% of each run, Pallas kernels for 0% -> 27%
where the time goes in v1:
time: 192 us; the launch traced here: 189 us
  Pallas kernels  162 us (84%)
  between operations  14.1 us (7%)
  local copies, waits for them, and re-layouts  7.23 us (4%)
  waiting for transfers between devices  5.54 us (3%)
    pallas_call x1, Pallas kernels, reduce(): pl.pallas_call(reduce_kernel, out_shape=(jax.ShapeDtypeStruct((ROWS, D),...  57.7 us
    pallas_call x1, Pallas kernels, deal(): pl.pallas_call(deal_kernel, out_shape=(jax.ShapeDtypeStruct((NC, SLOTS, T...  46.5 us
    pallas_call x1, Pallas kernels, slopes(): pl.pallas_call(slope_kernel, out_shape=(jax.ShapeDtypeStruct((ROWS, D), F...  22.2 us
    pallas_call x1, Pallas kernels, backward(): pl.pallas_call(backward_kernel, out_shape=(jax.ShapeDtypeStruct((NZ, NX,...  17.7 us
    pallas_call x1, Pallas kernels, forward(): pl.pallas_call(forward_kernel, out_shape=(jax.ShapeDtypeStruct((REL, D, D...  14 us
    all_gather x1, waiting for transfers between devices, shards(): full = lax.all_gather(weights, 'fsdp', axis=1, tiled=True)  4.86 us
    pallas_call x1, Pallas kernels, pack(): pl.pallas_call(pack_kernel, out_shape=(jax.ShapeDtypeStruct((NC, SLOTS, T...  4.33 us
    unnamed x5, local copies, waits for them, and re-layouts  4.22 us
  transfers between devices with their start and end apart: 1, of which 1 were waited for; matrix products, arithmetic and copies ran while one was open for 1% of the time, Pallas kernels for 27%

profile of v1, /device:TPU:24, one launch (start us, length us, event | category | flops | bytes accessed | tf_op | source)
XLA Modules:
  0.0 189.2 jit_solution(16285812285817435074)
XLA Ops:
  7.2 0.0 all-gather.2.cloned.1.call-start
  7.2 0.7 all-gather.2.cloned.1.call-update
  7.9 4.3 %shard_map.112 = (bf16[8,8,128,128]{3,2,1,0:T(8,128)(2,1)}, s32[8,8,128]{2,1,0:T(8,128)}) custom-call(s32[32,48]{1,0:T(8,128)} %bitcast.13, s32[32,48]{1,0:T(8,128)} %bitcast.14, s32[32,48]{1,0:T(8,128)} %bitcast.15, s32[32,48]{1,0:T(8,128)} %bitcast.16, s32[32]{0:T(128)} %bitcast.17, bf16[48,128,128]{2,1,0:T(8,128)(2,1)} %bitcast.11), custom_call_target="tpu_custom_call" | custom-call | tf_op jit(solution)/shard_map/pallas_call | solution.py:111
  12.2 46.5 %shard_map.113 = (bf16[8,8,128,128]{3,2,1,0:T(8,128)(2,1)}, s32[8,8,128]{2,1,0:T(8,128)}, bf16[8,4,64,512]{3,2,1,0:T(8,128)(2,1)}) custom-call(bf16[8,8,128,128]{3,2,1,0:T(8,128)(2,1)} %get-tuple-element.17.packed, s32[8,8,128]{2,1,0:T(8,128)} %get-tuple-element.18.meta, bf16[512,512]{1,0:T(8,128)(2,1)} %states.1), custom_call_target="tpu_custom_call" | custom-call | tf_op jit(solution)/shard_map/pallas_call | solution.py:198
  58.7 1.5 constant_dynamic-slice_fusion
  60.2 4.9 %all-gather.2.cloned.1.call-done.weights = bf16[5,512,512]{2,1,0:T(8,128)(2,1)} async-done(((bf16[5,128,512]{2,1,0:T(8,128)(2,1)}), bf16[5,512,512]{2,1,0:T(8,128)(2,1)}) %all-gather.2.cloned.1.call-update) | async-done | bytes 2621456 | tf_op jit(solution)/shard_map/all_gather | solution.py:560
  65.1 14.0 %shard_map.114 = (bf16[4,512,512]{2,1,0:T(8,128)(2,1)}, bf16[8,64,512]{2,1,0:T(8,128)(2,1)}) custom-call(s32[8,8,128]{2,1,0:T(8,128)} %get-tuple-element.19.meta, bf16[8,8,128,128]{3,2,1,0:T(8,128)(2,1)} %get-tuple-element.20.tiles, bf16[2048,512]{1,0:T(8,128)(2,1)} %bitcast.10, bf16[5,512,512]{2,1,0:T(8,128)(2,1)} %all-gather.2.cloned.1.call-done.weights), custom_call_target="tpu_custom_call" | custom-call | tf_op jit(solution)/shard_map/pallas_call | solution.py:242
  79.1 22.2 %shard_map.115 = (f32[64,512]{1,0:T(8,128)}, bf16[8,64,512]{2,1,0:T(8,128)(2,1)}, f32[64,512]{1,0:T(8,128)}) custom-call(bf16[8,64,512]{2,1,0:T(8,128)(2,1)} %get-tuple-element.22.m_in, bf16[64,512]{1,0:T(8,128)(2,1)} %get-tuple-element.32.x_own, bf16[64,512]{1,0:T(8,128)(2,1)} %get-tuple-element.31.cot_own, ...), custom_call_target="tpu_custom_call" | custom-call | tf_op jit(solution)/shard_map/pallas_call | solution.py:292
  101.2 1.5 dynamic-slice_bitcast_fusion.s_own
  102.7 17.7 %shard_map.116 = (bf16[8,4,64,512]{3,2,1,0:T(8,128)(2,1)}, bf16[8,8,160,128]{3,2,1,0:T(8,128)(2,1)}) custom-call(s32[8,8,128]{2,1,0:T(8,128)} %get-tuple-element.19.meta, bf16[8,8,128,128]{3,2,1,0:T(8,128)(2,1)} %get-tuple-element.20.tiles, bf16[512,512]{1,0:T(8,128)(2,1)} %bitcast.12, bf16[5,512,512]{2,1,0:T(8,128)(2,1)} %all-gather.2.cloned.1.call-done.weights, ...), custom_call_target="tpu_custom_call" | custom-call | tf_op jit(solution)/shard_map/pallas_call | solution.py:356
  120.4 0.0 copy-start
  120.4 57.7 %shard_map.117 = (f32[64,512]{1,0:T(8,128)}, f32[5,64,512]{2,1,0:T(8,128)}) custom-call(bf16[8,4,64,512]{3,2,1,0:T(8,128)(2,1)} %get-tuple-element.26.g_in, bf16[8,8,160,128]{3,2,1,0:T(8,128)(2,1)} %get-tuple-element.27.w_in, f32[64,512]{1,0:T(8,128)} %get-tuple-element.28.self_in), custom_call_target="tpu_custom_call" | custom-call | tf_op jit(solution)/shard_map/pallas_call | solution.py:516
  178.1 0.0 copy-done
  178.2 0.7 copy.15
  178.8 1.6 copy.16
  180.4 2.0 %copy.17 = f32[5,64,512]{2,1,0:T(8,128)} copy(f32[5,64,512]{2,1,0:T(8,128)} %get-tuple-element.38) | data formatting | bytes 1310720
Async XLA Ops:
  7.2 57.9 %all-gather.2.cloned.1.call-start = ((), (), s32[]{:S(2)}) async-start(), calls=%async_computation | async-start | bytes 3276800 | tf_op jit(solution)/shard_map/all_gather | solution.py:560
  120.4 57.8 %copy-start = (f32[64,512]{1,0:T(8,128)S(1)}, f32[64,512]{1,0:T(8,128)}, u32[]{:S(2)}) copy-start(f32[64,512]{1,0:T(8,128)} %get-tuple-element.36) | copy-start | bytes 393220
Sparse Core Ops, SparseCore 0:
  9.8 55.2 all-gather.1

commit v2 on v1

v2 whole, which is shorter than its diff:
```python
import jax
import jax.numpy as jnp
from jax import lax
from jax.experimental import pallas as pl
from jax.experimental.pallas import tpu as pltpu
from jax.sharding import PartitionSpec as P

D = 512
REL = 4
TILE = 128
EB = 48
NZ = 8
NX = 4
NY = 4
NC = 8
SLOTS = 8
ROWS = 64
WROWS = 320
WC = 128
BF = jnp.bfloat16
F32 = jnp.float32
MESH = pl.DeviceIdType.MESH
ANY = pl.BlockSpec(memory_space=pl.ANY)
VM = pl.BlockSpec(memory_space=pltpu.VMEM)
SM = pl.BlockSpec(memory_space=pltpu.SMEM)
DMA = pltpu.SemaphoreType.DMA


def params(mib, collective=None):
    more = {} if collective is None else {"collective_id": collective, "has_side_effects": True}
    return pltpu.CompilerParams(vmem_limit_bytes=mib * 1024 * 1024, **more)


def place():
    g = lax.axis_index("graph")
    return g // NX, g % NX, lax.axis_index("fsdp"), lax.axis_index("replica")


def send(src, dst, ssem, rsem, z, x, y, p):
    return pltpu.make_async_remote_copy(
        src_ref=src,
        dst_ref=dst,
        send_sem=ssem,
        recv_sem=rsem,
        device_id=(z * NX + x, y, p),
        device_id_type=MESH,
    )


def greet(partners, swap=None):
    barrier = pltpu.get_barrier_semaphore()
    for z, x, y, p in partners:
        pl.semaphore_signal(barrier, inc=1, device_id=(z * NX + x, y, p), device_id_type=MESH)
    if swap is not None:
        (z, x, y, p), is_self = swap

        @pl.when(jnp.logical_not(is_self))
        def _():
            pl.semaphore_signal(barrier, inc=1, device_id=(z * NX + x, y, p), device_id_type=MESH)

        pl.semaphore_wait(barrier, len(partners) + jnp.where(is_self, 0, 1))
    else:
        pl.semaphore_wait(barrier, len(partners))


def group_peers(z, x, y, p):
    return [
        (z, x, (y + dy) % NY, (p + dp) % 2)
        for dy, dp in ((0, 1), (1, 0), (3, 0), (1, 1), (3, 1), (2, 0), (2, 1))
    ]


def y_peers(z, x, y, p):
    return [(z, x, (y + i) % NY, p) for i in (1, 3, 2)]


def x_peers(z, x, y, p):
    return [(z, (x + i) % NX, y, p) for i in (1, 2, 3)]


def z_peers(z, x, y, p, steps=(1, 7)):
    return [((z + i) % NZ, x, y, p) for i in steps]


def swap_of(z, x, y, p):
    return (2 * (z // 2) + p, y, x, z % 2), (x == y) & (z % 2 == p)


def pack_kernel(owner, source, target, relation, count, tiles, packed, meta, filled):
    g = lax.axis_index("graph")
    for c in range(NC):
        for s in range(SLOTS):
            meta[c, 0, s] = -1

    def clear(o, carry):
        filled[o] = 0
        return carry

    lax.fori_loop(0, NZ * NX, clear, 0)

    def put(e, carry):
        o = owner[g, e]
        rank = filled[o]
        filled[o] = rank + 1
        c = (o % NX) * 2 + (o // NX) % 2
        s = (o // 8) * 2 + rank
        meta[c, 0, s] = source[g, e] + 4 * target[g, e] + 16 * relation[g, e]
        packed[c, s] = tiles[e]
        return carry

    lax.fori_loop(0, count[g], put, 0)


def pack(owner, source, target, relation, count, tiles):
    return pl.pallas_call(
        pack_kernel,
        out_shape=(
            jax.ShapeDtypeStruct((NC, SLOTS, TILE, TILE), BF),
            jax.ShapeDtypeStruct((NC, 8, 128), jnp.int32),
        ),
        in_specs=[SM] * 5 + [VM],
        out_specs=(VM, SM),
        scratch_shapes=[pltpu.SMEM((NZ * NX,), jnp.int32)],
        compiler_params=params(8),
    )(owner, source, target, relation, count, tiles)


def deal_kernel(
    packed, meta, states, weights, tiles_o, meta_o, xp, full,
    own_sems, t_send, t_recv, m_send, m_recv, v_send, v_recv, x_send, x_recv, z_send, z_recv,
    wy_send, wy_recv, wx_send, wx_recv, wc_send, wc_recv,
):
    z, x, y, p = place()
    peers = group_peers(z, x, y, p)
    core, ys = peers[0], y_peers(z, x, y, p)
    xs = x_peers(z, x, y, p)
    up, down = z_peers(z, x, y, p)
    target, is_self = swap_of(z, x, y, p)
    greet(peers + xs + [up, down], (target, is_self))
    c = y * 2 + p
    piece = states.at[pl.ds(pl.multiple_of((p * NY + y) * ROWS, ROWS), ROWS)]

    @pl.when(jnp.logical_not(is_self))
    def _():
        send(piece, xp.at[target[0], target[1]], v_send, v_recv, *target).start()

    @pl.when(is_self)
    def _():
        pltpu.make_async_copy(piece, xp.at[z, x], own_sems.at[0]).start()

    def rows(yi, xi):
        return pl.ds(pl.multiple_of(yi * 128 + p * 64 + xi * 16, 16), 16)

    wy_copies = []
    mine_w = weights.at[:, pl.ds(pl.multiple_of(p * 64 + x * 16, 16), 16)]
    for i, q in enumerate(ys):
        a = send(mine_w, full.at[:, rows(y, x)], wy_send.at[i], wy_recv.at[i], *q)
        a.start()
        wy_copies.append(a)

    own_copies = [
        pltpu.make_async_copy(packed.at[c], tiles_o.at[c], own_sems.at[1]),
        pltpu.make_async_copy(meta.at[c], meta_o.at[c], own_sems.at[2]),
        pltpu.make_async_copy(
            weights, full.at[:, pl.ds(pl.multiple_of(y * 128, 128), 128)], own_sems.at[3]
        ),
    ]
    for a in own_copies:
        a.start()
    tile_copies = []
    for i, q in enumerate(peers):
        cq = q[2] * 2 + q[3]
        a = send(packed.at[cq], tiles_o.at[c], t_send.at[i], t_recv.at[i], *q)
        b = send(meta.at[cq], meta_o.at[c], m_send.at[i], m_recv.at[i], *q)
        a.start()
        b.start()
        tile_copies += [a, b]

    @pl.when(jnp.logical_not(is_self))
    def _():
        send(piece, xp.at[z, x], v_send, v_recv, *target).wait()

    @pl.when(is_self)
    def _():
        pltpu.make_async_copy(piece, xp.at[z, x], own_sems.at[0]).wait()

    x_copies = [
        send(xp.at[z, x], xp.at[z, x], x_send.at[i], x_recv.at[i], *q) for i, q in enumerate(xs)
    ]
    for a in x_copies:
        a.start()

    wx_copies = []
    wc_copies = []
    z_copies = {}
    for s in range(4):
        for i in range(NX):
            xi = (x + i) % NX
            if s == 0 and i > 0:
                x_copies[3 - i].wait_recv()
            for d, q in ((0, up), (1, down)):
                if s > 0 and (d, s - 1, i) in z_copies:
                    z_copies[d, s - 1, i].wait_recv()
                if s < 3 or (i < 2) == (d == 0):
                    zs = (z - s + NZ) % NZ if d == 0 else (z + s) % NZ
                    a = send(xp.at[zs, xi], xp.at[zs, xi], z_send.at[d, s, i], z_recv.at[d, s, i], *q)
                    a.start()
                    z_copies[d, s, i] = a
        if s == 0:
            for i, yi in enumerate(((y + 3) % NY, (y + 1) % NY, (y + 2) % NY)):
                wy_copies[i].wait_recv()
                for j, q in enumerate(xs):
                    ref = full.at[:, rows(yi, x)]
                    a = send(ref, ref, wx_send.at[i, j], wx_recv.at[i, j], *q)
                    a.start()
                    wx_copies.append(a)
        if s == 2:
            for i, yi in enumerate(((y + 3) % NY, (y + 1) % NY, (y + 2) % NY)):
                for j in range(3):
                    wx_copies[i * 3 + j].wait_recv()
                ref = full.at[:, pl.ds(pl.multiple_of(yi * 128 + p * 64, 64), 64)]
                a = send(ref, ref, wc_send.at[i], wc_recv.at[i], *core)
                a.start()
                wc_copies.append(a)
    for (d, s, i), a in z_copies.items():
        if s == 3:
            a.wait_recv()
    for a in x_copies + list(z_copies.values()) + wy_copies + wx_copies:
        a.wait_send()
    for a in own_copies + wc_copies + tile_copies:
        a.wait()


def deal(packed, meta, states, weights):
    return pl.pallas_call(
        deal_kernel,
        out_shape=(
            jax.ShapeDtypeStruct((NC, SLOTS, TILE, TILE), BF),
            jax.ShapeDtypeStruct((NC, 8, 128), jnp.int32),
            jax.ShapeDtypeStruct((NZ, NX, ROWS, D), BF),
            jax.ShapeDtypeStruct((REL + 1, D, D), BF),
        ),
        in_specs=[ANY] * 4,
        out_specs=(ANY,) * 4,
        scratch_shapes=[
            DMA((4,)), DMA((7,)), DMA((7,)), DMA((7,)), DMA((7,)), DMA(()), DMA(()),
            DMA((3,)), DMA((3,)), DMA((2, 4, 4)), DMA((2, 4, 4)),
            DMA((3,)), DMA((3,)), DMA((3, 3)), DMA((3, 3)), DMA((3,)), DMA((3,)),
        ],
        compiler_params=params(1, 0),
    )(packed, meta, states, weights)


def forward_kernel(meta, tiles, xp, weights, t_out, m_out, acc):
    acc[...] = jnp.zeros_like(acc)

    def slot(i, carry):
        c = i // SLOTS
        s = i % SLOTS
        code = meta[c, 0, s]

        @pl.when(code >= 0)
        def _():
            source = pl.multiple_of(((s // 2) * 4 + code % 4) * TILE, TILE)
            into = pl.multiple_of((code // 4) * TILE, TILE)
            got = jnp.dot(tiles[c, s], xp[pl.ds(source, TILE), :], preferred_element_type=F32)
            acc[pl.ds(into, TILE), :] += got

        return carry

    lax.fori_loop(0, NC * SLOTS, slot, 0)
    total = jnp.zeros((D, D), F32)
    for r in range(REL):
        t = acc[r * D : (r + 1) * D, :].astype(BF)
        t_out[r] = t
        total = total + jnp.dot(t, weights[r], preferred_element_type=F32)
    total = total.astype(BF)
    for c in range(NC):
        m_out[c % 2, c // 2] = total[c * ROWS : (c + 1) * ROWS]


def forward(meta, tiles, xp, weights):
    return pl.pallas_call(
        forward_kernel,
        out_shape=(
            jax.ShapeDtypeStruct((REL, D, D), BF),
            jax.ShapeDtypeStruct((2, NY, ROWS, D), BF),
        ),
        in_specs=[SM, VM, VM, VM],
        out_specs=(VM, VM),
        scratch_shapes=[pltpu.VMEM((REL * D, D), F32)],
        compiler_params=params(24),
    )(meta, tiles, xp, weights)


def slope_kernel(
    m_in, states, cotangent, weights, out_o, slope_o, self_o,
    x_own, cot_own, w_self, c_buf, y_src, y_buf,
    own_sems, c_s, c_r, y_s, y_r, s_s, s_r, f_s, f_r,
):
    z, x, y, p = place()
    core, ys = (z, x, y, 1 - p), y_peers(z, x, y, p)
    c = y * 2 + p
    share = pl.ds(pl.multiple_of(c * ROWS, ROWS), ROWS)
    loads = [
        pltpu.make_async_copy(states.at[share], x_own, own_sems.at[0]),
        pltpu.make_async_copy(cotangent.at[share], cot_own, own_sems.at[1]),
        pltpu.make_async_copy(weights.at[REL], w_self, own_sems.at[2]),
    ]
    for a in loads:
        a.start()
    greet([core] + ys)
    across = send(m_in.at[1 - p], c_buf, c_s, c_r, *core)
    across.start()
    for a in loads:
        a.wait()
    pre = jnp.dot(x_own[...], w_self[...], preferred_element_type=F32)
    across.wait_recv()
    y_copies = []
    for i, q in enumerate(ys):
        y_src[i] = (m_in[p, q[2]].astype(F32) + c_buf[q[2]].astype(F32)).astype(BF)
        a = send(y_src.at[i], y_buf.at[i], y_s.at[i], y_r.at[i], *q)
        a.start()
        y_copies.append(a)
    pre = pre + m_in[p, y].astype(F32) + c_buf[y].astype(F32)
    for i, a in enumerate(y_copies):
        a.wait_recv()
        pre = pre + y_buf[i].astype(F32)
    sigma = jax.nn.sigmoid(pre)
    slope = (cot_own[...].astype(F32) * (sigma * (1.0 + pre * (1.0 - sigma)))).astype(BF)
    slope_o[c] = slope
    mine = slope_o.at[c]
    s_copies = []
    for i, q in enumerate(ys + [core]):
        a = send(mine, mine, s_s.at[i], s_r.at[i], *q)
        a.start()
        s_copies.append(a)
    out_o[...] = pre * sigma
    self_o[...] = lax.dot_general(
        slope, w_self[...], (((1,), (1,)), ((), ())), preferred_element_type=F32
    )
    f_copies = []
    for i, yi in enumerate(((y + 3) % NY, (y + 1) % NY, (y + 2) % NY)):
        s_copies[i].wait_recv()
        ref = slope_o.at[yi * 2 + p]
        a = send(ref, ref, f_s.at[i], f_r.at[i], *core)
        a.start()
        f_copies.append(a)
    s_copies[3].wait_recv()
    for a in [across] + y_copies + s_copies:
        a.wait_send()
    for a in f_copies:
        a.wait()


def slopes(m_in, states, cotangent, weights):
    return pl.pallas_call(
        slope_kernel,
        out_shape=(
            jax.ShapeDtypeStruct((ROWS, D), F32),
            jax.ShapeDtypeStruct((NC, ROWS, D), BF),
            jax.ShapeDtypeStruct((ROWS, D), F32),
        ),
        in_specs=[VM, ANY, ANY, ANY],
        out_specs=(VM, VM, VM),
        scratch_shapes=[
            pltpu.VMEM((ROWS, D), BF), pltpu.VMEM((ROWS, D), BF), pltpu.VMEM((D, D), BF),
            pltpu.VMEM((NY, ROWS, D), BF), pltpu.VMEM((3, ROWS, D), BF), pltpu.VMEM((3, ROWS, D), BF),
            DMA((3,)), DMA(()), DMA(()), DMA((3,)), DMA((3,)), DMA((4,)), DMA((4,)), DMA((3,)), DMA((3,)),
        ],
        compiler_params=params(8, 1),
    )(m_in, states, cotangent, weights)


def backward_kernel(meta, tiles, slope, weights, t_in, states, g_out, w_out, zs, acc):
    over_rows = (((0,), (0,)), ((), ()))
    over_columns = (((1,), (1,)), ((), ()))
    share = lax.axis_index("fsdp") * 2 + lax.axis_index("replica")
    share = pl.ds(pl.multiple_of(share * ROWS, ROWS), ROWS)
    acc[...] = jnp.zeros_like(acc)
    for r in range(REL):
        zs[r * D : (r + 1) * D, :] = lax.dot_general(
            slope[...], weights[r], over_columns, preferred_element_type=F32
        ).astype(BF)

    def slot(i, carry):
        c = i // SLOTS
        s = i % SLOTS
        code = meta[c, 0, s]

        @pl.when(code >= 0)
        def _():
            into = pl.multiple_of(((s // 2) * 4 + code % 4) * TILE, TILE)
            source = pl.multiple_of((code // 4) * TILE, TILE)
            got = lax.dot_general(
                tiles[c, s], zs[pl.ds(source, TILE), :], over_rows, preferred_element_type=F32
            )
            acc[pl.ds(into, TILE), :] += got

        return carry

    lax.fori_loop(0, NC * SLOTS, slot, 0)
    for k in range(4):
        for b in range(4):
            for h in range(2):
                row = (k * 4 + b) * TILE + h * ROWS
                g_out[2 * k + h, b] = acc[row : row + ROWS, :].astype(BF)
    for m in range(REL + 1):
        if m < REL:
            part = lax.dot_general(t_in[m], slope[...], over_rows, preferred_element_type=F32)
        else:
            part = lax.dot_general(
                states[share, :], slope[share, :], over_rows, preferred_element_type=F32
            )
        part = part.astype(BF)
        for c in range(NC):
            for q in range(NX):
                w_out[c % 2, c // 2, q, m * ROWS : (m + 1) * ROWS, :] = part[
                    c * ROWS : (c + 1) * ROWS, q * WC : (q + 1) * WC
                ]


def backward(meta, tiles, slope, weights, t_in, states):
    return pl.pallas_call(
        backward_kernel,
        out_shape=(
            jax.ShapeDtypeStruct((NZ, NX, ROWS, D), BF),
            jax.ShapeDtypeStruct((2, NY, NX, WROWS, WC), BF),
        ),
        in_specs=[SM] + [VM] * 5,
        out_specs=(VM, VM),
        scratch_shapes=[pltpu.VMEM((REL * D, D), BF), pltpu.VMEM((16 * TILE, D), F32)],
        compiler_params=params(28),
    )(meta, tiles, slope, weights, t_in, states)


def reduce_kernel(
    g_in, w_in, v_buf, w_out,
    c_buf, y_src, y_buf, xw_src, xw_buf, zw_src, zw_buf, aw_buf,
    g_src, g_buf, gx_src, gx_buf, v_src,
    c_s, c_r, y_s, y_r, xw_s, xw_r, zw_s, zw_r, aw_s, aw_r, bw_s, bw_r,
    g_s, g_r, gx_s, gx_r, v_s, v_r,
):
    z, x, y, p = place()
    core = (z, x, y, 1 - p)
    ys = y_peers(z, x, y, p)
    xs = x_peers(z, x, y, p)
    around = z_peers(z, x, y, p, (4, 3, 5, 2, 6, 1, 7))
    up, down = around[5], around[6]
    target, is_self = swap_of(z, x, y, p)
    greet([core] + ys + xs + around, (target, is_self))

    order = (1, 2, 3, 0)
    c_copies = []
    for i in order:
        xi = (x + i) % NX
        a = send(w_in.at[1 - p, :, xi], c_buf.at[:, xi], c_s.at[i], c_r.at[i], *core)
        a.start()
        c_copies.append(a)

    g_copies = {}
    hops = {(d, i): 4 if (i < 2) == (d == 0) else 3 for d in range(2) for i in range(NX)}

    def chain(s):
        for i in range(NX):
            xi = (x + i) % NX
            for d, q in ((0, up), (1, down)):
                left = hops[d, i] - s
                if left <= 0:
                    continue
                zd = (z + left) % NZ if d == 0 else (z - left + NZ) % NZ
                if s == 0:
                    src = g_in.at[zd, xi]
                else:
                    g_copies[d, s - 1, i].wait_recv()
                    g_src[d, s - 1, i] = (
                        g_in[zd, xi].astype(F32) + g_buf[d, s - 1, i].astype(F32)
                    ).astype(BF)
                    src = g_src.at[d, s - 1, i]
                a = send(src, g_buf.at[d, s, i], g_s.at[d, s, i], g_r.at[d, s, i], *q)
                a.start()
                g_copies[d, s, i] = a

    chain(0)
    y_copies = {}
    for n, i in enumerate(order):
        xi = (x + i) % NX
        c_copies[n].wait_recv()
        for j, q in enumerate(ys):
            yi = q[2]
            y_src[i, j] = (w_in[p, yi, xi].astype(F32) + c_buf[yi, xi].astype(F32)).astype(BF)
            a = send(y_src.at[i, j], y_buf.at[i, j], y_s.at[i, j], y_r.at[i, j], *q)
            a.start()
            y_copies[i, j] = a

    def y_total(i):
        xi = (x + i) % NX
        total = w_in[p, y, xi].astype(F32) + c_buf[y, xi].astype(F32)
        for j in range(3):
            y_copies[i, j].wait_recv()
            total = total + y_buf[i, j].astype(F32)
        return total

    chain(1)
    xw_copies = []

    def to_x(i):
        xw_src[i - 1] = y_total(i).astype(BF)
        a = send(xw_src.at[i - 1], xw_buf.at[i - 1], xw_s.at[i - 1], xw_r.at[i - 1], *xs[i - 1])
        a.start()
        xw_copies.append(a)

    to_x(1)
    to_x(2)
    chain(2)
    to_x(3)
    total = y_total(0)
    for i, a in enumerate(xw_copies):
        a.wait_recv()
        total = total + xw_buf[i].astype(F32)
    zw_src[...] = total.reshape(NZ, WROWS // NZ, WC)
    zw_copies = []
    for i, q in enumerate(around):
        a = send(zw_src.at[q[0]], zw_buf.at[i], zw_s.at[i], zw_r.at[i], *q)
        a.start()
        zw_copies.append(a)
    chain(3)

    mine = zw_src[z]
    for i, a in enumerate(zw_copies):
        a.wait_recv()
        mine = mine + zw_buf[i]
    aw_buf[z] = mine
    aw_copies = []
    for i, q in enumerate(around):
        a = send(aw_buf.at[z], aw_buf.at[z], aw_s.at[i], aw_r.at[i], *q)
        a.start()
        aw_copies.append(a)

    gx_copies = []
    own = None
    for i in order:
        xi = (x + i) % NX
        part = g_in[z, xi].astype(F32)
        for d in range(2):
            last = hops[d, i] - 1
            g_copies[d, last, i].wait_recv()
            part = part + g_buf[d, last, i].astype(F32)
        if i:
            gx_src[i - 1] = part.astype(BF)
            a = send(gx_src.at[i - 1], gx_buf.at[i - 1], gx_s.at[i - 1], gx_r.at[i - 1], *xs[i - 1])
            a.start()
            gx_copies.append(a)
        else:
            own = part

    for a in aw_copies:
        a.wait_recv()
    w_out[x] = aw_buf[...].reshape(WROWS, WC).astype(BF)
    bw_copies = []
    for i, q in enumerate(xs):
        a = send(w_out.at[x], w_out.at[x], bw_s.at[i], bw_r.at[i], *q)
        a.start()
        bw_copies.append(a)

    for i, a in enumerate(gx_copies):
        a.wait_recv()
        own = own + gx_buf[i].astype(F32)
    v_src[...] = own.astype(BF)

    @pl.when(jnp.logical_not(is_self))
    def _():
        a = send(v_src, v_buf, v_s, v_r, *target)
        a.start()
        a.wait()

    @pl.when(is_self)
    def _():
        v_buf[...] = v_src[...]

    for a in bw_copies:
        a.wait()
    for a in c_copies + zw_copies + xw_copies + aw_copies + gx_copies:
        a.wait_send()
    for a in list(y_copies.values()) + list(g_copies.values()):
        a.wait_send()


def reduce(g_in, w_in):
    return pl.pallas_call(
        reduce_kernel,
        out_shape=(
            jax.ShapeDtypeStruct((ROWS, D), BF),
            jax.ShapeDtypeStruct((NX, WROWS, WC), BF),
        ),
        in_specs=[VM] * 2,
        out_specs=(VM, VM),
        scratch_shapes=[
            pltpu.VMEM((NY, NX, WROWS, WC), BF),
            pltpu.VMEM((NX, 3, WROWS, WC), BF),
            pltpu.VMEM((NX, 3, WROWS, WC), BF),
            pltpu.VMEM((3, WROWS, WC), BF),
            pltpu.VMEM((3, WROWS, WC), BF),
            pltpu.VMEM((NZ, WROWS // NZ, WC), F32),
            pltpu.VMEM((7, WROWS // NZ, WC), F32),
            pltpu.VMEM((NZ, WROWS // NZ, WC), F32),
            pltpu.VMEM((2, 3, NX, ROWS, D), BF),
            pltpu.VMEM((2, 4, NX, ROWS, D), BF),
            pltpu.VMEM((3, ROWS, D), BF),
            pltpu.VMEM((3, ROWS, D), BF),
            pltpu.VMEM((ROWS, D), BF),
            DMA((4,)), DMA((4,)), DMA((4, 3)), DMA((4, 3)), DMA((3,)), DMA((3,)), DMA((7,)), DMA((7,)),
            DMA((7,)), DMA((7,)), DMA((3,)), DMA((3,)), DMA((2, 4, 4)), DMA((2, 4, 4)),
            DMA((3,)), DMA((3,)), DMA(()), DMA(()),
        ],
        compiler_params=params(28, 2),
    )(g_in, w_in)


def close_kernel(layer, own, v, w, layer_o, g_o, w_o):
    layer_o[...] = layer[...]
    g_o[...] = own[...] + v[...].astype(F32)
    for m in range(REL + 1):
        for q in range(NX):
            w_o[m, :, q * WC : (q + 1) * WC] = w[q, m * ROWS : (m + 1) * ROWS, :].astype(F32)


def close(layer, own, v, w):
    return pl.pallas_call(
        close_kernel,
        out_shape=(
            jax.ShapeDtypeStruct((ROWS, D), F32),
            jax.ShapeDtypeStruct((ROWS, D), F32),
            jax.ShapeDtypeStruct((REL + 1, ROWS, D), F32),
        ),
        in_specs=[VM] * 4,
        out_specs=(VM, VM, VM),
        compiler_params=params(8),
    )(layer, own, v, w)


def shards(
    states,
    weights,
    edge_tiles,
    edge_owner,
    edge_source,
    edge_target,
    edge_relation,
    edge_count,
    cotangent,
):
    groups = edge_owner.shape[0]
    owner = edge_owner.reshape(groups, EB)
    source = edge_source.reshape(groups, EB)
    target = edge_target.reshape(groups, EB)
    relation = edge_relation.reshape(groups, EB)
    count = edge_count.reshape(groups)
    tiles = edge_tiles.reshape(EB, TILE, TILE)
    packed, meta = pack(owner, source, target, relation, count, tiles)
    tiles, meta, xp, full = deal(packed, meta, states, weights)
    t_all, m_part = forward(meta, tiles, xp.reshape(-1, D), full)
    layer, slope, own = slopes(m_part, states, cotangent, full)
    g_part, w_part = backward(meta, tiles, slope.reshape(-1, D), full, t_all, states)
    v, w = reduce(g_part, w_part)
    return close(layer, own, v, w)


def solution(mesh):
    return jax.shard_map(
        shards,
        mesh=mesh,
        in_specs=(
            P("graph", None),
            P(None, "fsdp", None),
            P("graph", "fsdp", "replica", None, None, None),
            P(None, "fsdp", "replica", None),
            P(None, "fsdp", "replica", None),
            P(None, "fsdp", "replica", None),
            P(None, "fsdp", "replica", None),
            P(None, "fsdp", "replica"),
            P("graph", None),
        ),
        out_specs=(
            P(("graph", "fsdp", "replica"), None),
            P(("graph", "fsdp", "replica"), None),
            P(None, ("fsdp", "replica"), None),
        ),
        check_vma=False,
    )
```

time: 192 us -> 140 us (0.73)
  Pallas kernels: 162 us -> 131 us
  between operations: 14.1 us -> 0.73 us
  waiting for transfers between devices: 5.54 us -> 0 us
    pallas_call x1, Pallas kernels: 57.7 us -> 48 us  [reduce(): pl.pallas_call(reduce_kernel, out_shape=(jax.ShapeDtypeStruct((ROWS, D),...]
    pallas_call x1, Pallas kernels: 22.2 us -> 14.6 us  [slopes(): pl.pallas_call(slope_kernel, out_shape=(jax.ShapeDtypeStruct((ROWS, D), F...]
    pallas_call x1, Pallas kernels: 46.5 us -> 39 us  [deal(): pl.pallas_call(deal_kernel, out_shape=(jax.ShapeDtypeStruct((NC, SLOTS, T...]
    all_gather x1 -> x0, waiting for transfers between devices: 4.86 us -> none  [shards(): full = lax.all_gather(weights, 'fsdp', axis=1, tiled=True)]
    pallas_call x1, Pallas kernels: 17.7 us -> 13.5 us  [backward(): pl.pallas_call(backward_kernel, out_shape=(jax.ShapeDtypeStruct((NZ, NX,...]
    pallas_call x1, Pallas kernels: 14 us -> 10.8 us  [forward(): pl.pallas_call(forward_kernel, out_shape=(jax.ShapeDtypeStruct((REL, D, D...]
    unnamed x5 -> x20, local copies, waits for them, and re-layouts: 4.22 us -> 7.06 us
  transfers between devices with their start and end apart: 1 -> 0, of which waited for: 1 -> 0; matrix products, arithmetic and copies ran while one was open for 1% -> 0% of each run, Pallas kernels for 27% -> 0%
where the time goes in v2:
time: 140 us; the launch traced here: 139 us
  Pallas kernels  131 us (94%)
  local copies, waits for them, and re-layouts  7.06 us (5%)
    pallas_call x1, Pallas kernels, reduce(): pl.pallas_call(reduce_kernel, out_shape=(jax.ShapeDtypeStruct((ROWS, D),...  48 us
    pallas_call x1, Pallas kernels, deal(): pl.pallas_call(deal_kernel, out_shape=(jax.ShapeDtypeStruct((NC, SLOTS, T...  39 us
    pallas_call x1, Pallas kernels, slopes(): pl.pallas_call(slope_kernel, out_shape=(jax.ShapeDtypeStruct((ROWS, D), F...  14.6 us
    pallas_call x1, Pallas kernels, backward(): pl.pallas_call(backward_kernel, out_shape=(jax.ShapeDtypeStruct((NZ, NX,...  13.5 us
    pallas_call x1, Pallas kernels, forward(): pl.pallas_call(forward_kernel, out_shape=(jax.ShapeDtypeStruct((REL, D, D...  10.8 us
    unnamed x20, local copies, waits for them, and re-layouts  7.06 us
    pallas_call x1, Pallas kernels, pack(): pl.pallas_call(pack_kernel, out_shape=(jax.ShapeDtypeStruct((NC, SLOTS, T...  3.93 us

profile of v2, /device:TPU:24, one launch (start us, length us, event | category | flops | bytes accessed | tf_op | source)
XLA Modules:
  0.0 138.5 jit_solution(8189555389207812805)
XLA Ops:
  0.6 0.0 copy-start.2
  0.6 1.4 %copy-done.2 = bf16[1,1,1,48,128,128]{5,4,3,2,1,0:T(8,128)(2,1)S(1)} copy-done((bf16[1,1,1,48,128,128]{5,4,3,2,1,0:T(8,128)(2,1)S(1)}, bf16[1,1,1,48,128,128]{5,4,3,2,1,0:T(8,128)(2,1)}, u32[]{:S(2)}) %copy-start.2) | copy-done | bytes 1572888
  2.0 0.0 copy-start.5
  2.0 0.7 copy-done.5
  2.8 0.0 copy-start.6
  2.8 0.7 copy-done.6
  3.5 0.0 copy-start.7
  3.5 0.7 copy-done.7
  4.2 0.0 copy-start.8
  4.2 0.7 copy-done.8
  4.9 0.0 copy-start.9
  4.9 0.7 copy-done.9
  5.6 3.9 %shard_map.112 = (bf16[8,8,128,128]{3,2,1,0:T(8,128)(2,1)S(1)}, s32[8,8,128]{2,1,0:T(8,128)S(1)}) custom-call(s32[32,48]{1,0:T(8,128)S(1)} %bitcast.11, s32[32,48]{1,0:T(8,128)S(1)} %bitcast.12, s32[32,48]{1,0:T(8,128)S(1)} %bitcast.13, s32[32,48]{1,0:T(8,128)S(1)} %bitcast.14, s32[32]{0:T(128)S(1)} %bitcast.15, bf16[48,128,128]{2,1,0:T(8,128)(2,1)S(1)} %bitcast.9), custom_call_target="tpu_custom_call" | custom-call | tf_op jit(solution)/shard_map/pallas_call | solution.py:115
  9.5 0.0 copy-start
  9.5 1.0 copy-done
  10.6 0.0 copy-start.3
  10.6 1.1 copy-done.3
  11.6 39.0 %shard_map.113 = (bf16[8,8,128,128]{3,2,1,0:T(8,128)(2,1)S(1)}, s32[8,8,128]{2,1,0:T(8,128)S(1)}, bf16[8,4,64,512]{3,2,1,0:T(8,128)(2,1)S(1)}, bf16[5,512,512]{2,1,0:T(8,128)(2,1)S(1)}) custom-call(bf16[8,8,128,128]{3,2,1,0:T(8,128)(2,1)S(1)} %get-tuple-element.18.packed, s32[8,8,128]{2,1,0:T(8,128)S(1)} %get-tuple-element.19.meta, ...), custom_call_target="tpu_custom_call" | custom-call | tf_op jit(solution)/shard_map/pallas_call | solution.py:235
  50.7 0.0 copy-start.1
  50.7 0.0 copy-start.4
  50.7 10.8 %shard_map.114 = (bf16[4,512,512]{2,1,0:T(8,128)(2,1)S(1)}, bf16[2,4,64,512]{3,2,1,0:T(8,128)(2,1)S(1)}) custom-call(s32[8,8,128]{2,1,0:T(8,128)S(1)} %get-tuple-element.20.meta, bf16[8,8,128,128]{3,2,1,0:T(8,128)(2,1)S(1)} %get-tuple-element.21.tiles, bf16[2048,512]{1,0:T(8,128)(2,1)S(1)} %bitcast.8, bf16[5,512,512]{2,1,0:T(8,128)(2,1)S(1)} %get-tuple-element.23.weights), custom_call_target="tpu_custom_call" | custom-call | tf_op jit(solution)/shard_map/pallas_call | solution.py:283
  61.4 0.0 copy-done.1
  61.5 0.0 copy-done.4
  61.5 14.6 %shard_map.115 = (f32[64,512]{1,0:T(8,128)S(1)}, bf16[8,64,512]{2,1,0:T(8,128)(2,1)S(1)}, f32[64,512]{1,0:T(8,128)S(1)}) custom-call(bf16[2,4,64,512]{3,2,1,0:T(8,128)(2,1)S(1)} %get-tuple-element.24.m_in, bf16[512,512]{1,0:T(8,128)(2,1)S(1)} %copy-done.1, bf16[512,512]{1,0:T(8,128)(2,1)S(1)} %copy-done.4, bf16[5,512,512]{2,1,0:T(8,128)(2,1)S(1)} %get-tuple-element.23.weights), custom_call_target="tpu_custom_call" | custom-call | tf_op jit(solution)/shard_map/pallas_call | solution.py:357
  76.1 13.5 %shard_map.116 = (bf16[8,4,64,512]{3,2,1,0:T(8,128)(2,1)S(1)}, bf16[2,4,4,320,128]{4,3,2,1,0:T(8,128)(2,1)S(1)}) custom-call(s32[8,8,128]{2,1,0:T(8,128)S(1)} %get-tuple-element.20.meta, bf16[8,8,128,128]{3,2,1,0:T(8,128)(2,1)S(1)} %get-tuple-element.21.tiles, bf16[512,512]{1,0:T(8,128)(2,1)S(1)} %bitcast.10, ...), custom_call_target="tpu_custom_call" | custom-call | tf_op jit(solution)/shard_map/pallas_call | solution.py:424
  89.6 48.0 %shard_map.117 = (bf16[64,512]{1,0:T(8,128)(2,1)S(1)}, bf16[4,320,128]{2,1,0:T(8,128)(2,1)S(1)}) custom-call(bf16[8,4,64,512]{3,2,1,0:T(8,128)(2,1)S(1)} %get-tuple-element.29.g_in, bf16[2,4,4,320,128]{4,3,2,1,0:T(8,128)(2,1)S(1)} %get-tuple-element.30.w_in), custom_call_target="tpu_custom_call" | custom-call | tf_op jit(solution)/shard_map/pallas_call | solution.py:590
  137.5 1.0 shard_map.118
Async XLA Ops:
  0.6 1.4 %copy-start.2 = (bf16[1,1,1,48,128,128]{5,4,3,2,1,0:T(8,128)(2,1)S(1)}, bf16[1,1,1,48,128,128]{5,4,3,2,1,0:T(8,128)(2,1)}, u32[]{:S(2)}) copy-start(bf16[1,1,1,48,128,128]{5,4,3,2,1,0:T(8,128)(2,1)} %param.11) | copy-start | bytes 4718596
  2.0 0.7 copy-start.5
  2.8 0.7 copy-start.6
  3.5 0.7 copy-start.7
  4.2 0.7 copy-start.8
  4.9 0.7 copy-start.9
  9.5 1.0 copy-start
  10.6 1.1 copy-start.3
  50.7 10.8 %copy-start.1 = (bf16[512,512]{1,0:T(8,128)(2,1)S(1)}, bf16[512,512]{1,0:T(8,128)(2,1)}, u32[]{:S(2)}) copy-start(bf16[512,512]{1,0:T(8,128)(2,1)} %states.5) | copy-start | bytes 1572868
  50.7 10.8 %copy-start.4 = (bf16[512,512]{1,0:T(8,128)(2,1)S(1)}, bf16[512,512]{1,0:T(8,128)(2,1)}, u32[]{:S(2)}) copy-start(bf16[512,512]{1,0:T(8,128)(2,1)} %cotangent.1) | copy-start | bytes 1572868

commit v3 on v2

v3 whole, which is shorter than its diff:
```python
import jax
import jax.numpy as jnp
from jax import lax
from jax.experimental import pallas as pl
from jax.experimental.pallas import tpu as pltpu
from jax.sharding import PartitionSpec as P

D = 512
REL = 4
TILE = 128
EB = 48
NZ = 8
NX = 4
NY = 4
NC = 8
SLOTS = 8
ROWS = 64
WROWS = 320
WC = 128
BF = jnp.bfloat16
F32 = jnp.float32
MESH = pl.DeviceIdType.MESH
ANY = pl.BlockSpec(memory_space=pl.ANY)
VM = pl.BlockSpec(memory_space=pltpu.VMEM)
SM = pl.BlockSpec(memory_space=pltpu.SMEM)
HB = pl.BlockSpec(memory_space=pltpu.HBM)
DMA = pltpu.SemaphoreType.DMA


def params(mib, collective=None):
    more = {} if collective is None else {"collective_id": collective, "has_side_effects": True}
    return pltpu.CompilerParams(vmem_limit_bytes=mib * 1024 * 1024, **more)


def place():
    g = lax.axis_index("graph")
    return g // NX, g % NX, lax.axis_index("fsdp"), lax.axis_index("replica")


def send(src, dst, ssem, rsem, z, x, y, p):
    return pltpu.make_async_remote_copy(
        src_ref=src,
        dst_ref=dst,
        send_sem=ssem,
        recv_sem=rsem,
        device_id=(z * NX + x, y, p),
        device_id_type=MESH,
    )


def greet(partners, swap=None):
    barrier = pltpu.get_barrier_semaphore()
    for z, x, y, p in partners:
        pl.semaphore_signal(barrier, inc=1, device_id=(z * NX + x, y, p), device_id_type=MESH)
    count = len(partners)
    if swap is not None:
        (z, x, y, p), is_self = swap

        @pl.when(jnp.logical_not(is_self))
        def _():
            pl.semaphore_signal(barrier, inc=1, device_id=(z * NX + x, y, p), device_id_type=MESH)

        count = count + jnp.where(is_self, 0, 1)
    return lambda: pl.semaphore_wait(barrier, count)


def group_peers(z, x, y, p):
    return [
        (z, x, (y + dy) % NY, (p + dp) % 2)
        for dy, dp in ((0, 1), (1, 0), (3, 0), (1, 1), (3, 1), (2, 0), (2, 1))
    ]


def y_peers(z, x, y, p):
    return [(z, x, (y + i) % NY, p) for i in (1, 3, 2)]


def x_peers(z, x, y, p):
    return [(z, (x + i) % NX, y, p) for i in (1, 2, 3)]


def z_peers(z, x, y, p, steps=(1, 7)):
    return [((z + i) % NZ, x, y, p) for i in steps]


def swap_of(z, x, y, p):
    return (2 * (z // 2) + p, y, x, z % 2), (x == y) & (z % 2 == p)


def deal_kernel(
    owner, source, target_h, relation, count, tiles, states, weights, tiles_o, meta_o, xp, full,
    edges, counts, tiles_v, idx_v, idx, meta, packed,
    e_sems, own_sems, t_send, t_recv, m_send, m_recv, v_send, v_recv, x_send, x_recv, z_send, z_recv,
    wy_send, wy_recv, wx_send, wx_recv, wc_send, wc_recv,
):
    z, x, y, p = place()
    peers = group_peers(z, x, y, p)
    core, ys = peers[0], y_peers(z, x, y, p)
    xs = x_peers(z, x, y, p)
    up, down = z_peers(z, x, y, p)
    target, is_self = swap_of(z, x, y, p)
    arrived = greet(peers + xs + [up, down], (target, is_self))
    loads = [
        pltpu.make_async_copy(h, edges.at[i], e_sems.at[i])
        for i, h in enumerate((owner, source, target_h, relation))
    ]
    loads.append(pltpu.make_async_copy(count, counts, e_sems.at[4]))
    for a in loads:
        a.start()
    load_tiles = pltpu.make_async_copy(tiles, tiles_v, e_sems.at[5])
    load_tiles.start()
    c = y * 2 + p
    piece = states.at[pl.ds(pl.multiple_of((p * NY + y) * ROWS, ROWS), ROWS)]

    arrived()

    @pl.when(jnp.logical_not(is_self))
    def _():
        send(piece, xp.at[target[0], target[1]], v_send, v_recv, *target).start()

    @pl.when(is_self)
    def _():
        pltpu.make_async_copy(piece, xp.at[z, x], own_sems.at[0]).start()

    def rows(yi, xi):
        return pl.ds(pl.multiple_of(yi * 128 + p * 64 + xi * 16, 16), 16)

    wy_copies = []
    mine_w = weights.at[:, pl.ds(pl.multiple_of(p * 64 + x * 16, 16), 16)]
    for i, q in enumerate(ys):
        a = send(mine_w, full.at[:, rows(y, x)], wy_send.at[i], wy_recv.at[i], *q)
        a.start()
        wy_copies.append(a)

    own_w = pltpu.make_async_copy(
        weights, full.at[:, pl.ds(pl.multiple_of(y * 128, 128), 128)], own_sems.at[3]
    )
    own_w.start()

    for a in loads:
        a.wait()
    g = lax.axis_index("graph")
    e = lax.broadcasted_iota(jnp.int32, (NC * 4, EB), 1)
    row = lax.broadcasted_iota(jnp.int32, (NC * 4, EB), 0)
    wanted = (2 * (row & 3) + ((row >> 2) & 1)) * NX + (row >> 3)
    groups = lax.broadcasted_iota(jnp.int32, (1, NZ * NX), 1)
    live = jnp.sum(jnp.where(groups == g, counts[...], 0), axis=1, keepdims=True)
    own, src, dst, rel = (edges[i, pl.ds(g, 1), :] for i in range(4))
    code = src + 4 * (dst * REL + rel)
    hit = (own == wanted) & (e < live)
    first = jnp.min(jnp.where(hit, e, EB), axis=1, keepdims=True)
    last = jnp.max(jnp.where(hit, e, -1), axis=1, keepdims=True)
    code0 = jnp.sum(jnp.where(hit & (e == first), code, 0), axis=1, keepdims=True)
    code1 = jnp.sum(jnp.where(hit & (e == last), code, 0), axis=1, keepdims=True)
    code0 = jnp.where(first < EB, code0, -1)
    code1 = jnp.where(last > first, code1, -1)
    lane = lax.broadcasted_iota(jnp.int32, (NC * 4, 128), 1)
    idx_v[...] = jnp.where(lane == 0, jnp.minimum(first, EB - 1), jnp.maximum(last, 0))
    codes = jnp.where(lane == 0, code0, code1)
    meta[...] = jnp.full(meta.shape, -1, jnp.int32)
    for i in range(NC):
        meta[i, 0:4, :] = codes[i * 4 : i * 4 + 4]
    to_scalars = pltpu.make_async_copy(idx_v, idx, e_sems.at[6])
    to_scalars.start()
    to_scalars.wait()
    load_tiles.wait()

    def put(ci):
        def one(s, carry):
            packed[ci, s] = tiles_v[idx[ci * 4 + s // 2, s % 2]]
            return carry

        lax.fori_loop(0, SLOTS, one, 0)

    tile_copies = []
    for i, q in enumerate(peers):
        cq = q[2] * 2 + q[3]
        put(cq)
        a = send(packed.at[cq], tiles_o.at[c], t_send.at[i], t_recv.at[i], *q)
        b = send(meta.at[cq], meta_o.at[c], m_send.at[i], m_recv.at[i], *q)
        a.start()
        b.start()
        tile_copies += [a, b]
    put(c)
    own_copies = [
        pltpu.make_async_copy(packed.at[c], tiles_o.at[c], own_sems.at[1]),
        pltpu.make_async_copy(meta.at[c], meta_o.at[c], own_sems.at[2]),
    ]
    for a in own_copies:
        a.start()
    own_copies.append(own_w)

    @pl.when(jnp.logical_not(is_self))
    def _():
        send(piece, xp.at[z, x], v_send, v_recv, *target).wait()

    @pl.when(is_self)
    def _():
        pltpu.make_async_copy(piece, xp.at[z, x], own_sems.at[0]).wait()

    x_copies = [
        send(xp.at[z, x], xp.at[z, x], x_send.at[i], x_recv.at[i], *q) for i, q in enumerate(xs)
    ]
    for a in x_copies:
        a.start()

    wx_copies = []
    wc_copies = []
    z_copies = {}
    for s in range(4):
        for i in range(NX):
            xi = (x + i) % NX
            if s == 0 and i > 0:
                x_copies[3 - i].wait_recv()
            for d, q in ((0, up), (1, down)):
                if s > 0 and (d, s - 1, i) in z_copies:
                    z_copies[d, s - 1, i].wait_recv()
                if s < 3 or (i < 2) == (d == 0):
                    zs = (z - s + NZ) % NZ if d == 0 else (z + s) % NZ
                    a = send(xp.at[zs, xi], xp.at[zs, xi], z_send.at[d, s, i], z_recv.at[d, s, i], *q)
                    a.start()
                    z_copies[d, s, i] = a
        if s == 0:
            for i, yi in enumerate(((y + 3) % NY, (y + 1) % NY, (y + 2) % NY)):
                wy_copies[i].wait_recv()
                for j, q in enumerate(xs):
                    ref = full.at[:, rows(yi, x)]
                    a = send(ref, ref, wx_send.at[i, j], wx_recv.at[i, j], *q)
                    a.start()
                    wx_copies.append(a)
        if s == 2:
            for i, yi in enumerate(((y + 3) % NY, (y + 1) % NY, (y + 2) % NY)):
                for j in range(3):
                    wx_copies[i * 3 + j].wait_recv()
                ref = full.at[:, pl.ds(pl.multiple_of(yi * 128 + p * 64, 64), 64)]
                a = send(ref, ref, wc_send.at[i], wc_recv.at[i], *core)
                a.start()
                wc_copies.append(a)
    for (d, s, i), a in z_copies.items():
        if s == 3:
            a.wait_recv()
    for a in x_copies + list(z_copies.values()) + wy_copies + wx_copies:
        a.wait_send()
    for a in own_copies + wc_copies + tile_copies:
        a.wait()


def deal(owner, source, target, relation, count, tiles, states, weights):
    return pl.pallas_call(
        deal_kernel,
        out_shape=(
            jax.ShapeDtypeStruct((NC, SLOTS, TILE, TILE), BF),
            jax.ShapeDtypeStruct((NC, 8, 128), jnp.int32),
            jax.ShapeDtypeStruct((NZ, NX, ROWS, D), BF),
            jax.ShapeDtypeStruct((REL + 1, D, D), BF),
        ),
        in_specs=[HB] * 8,
        out_specs=(ANY,) * 4,
        scratch_shapes=[
            pltpu.VMEM((4, NZ * NX, EB), jnp.int32),
            pltpu.VMEM((1, NZ * NX), jnp.int32),
            pltpu.VMEM((EB, TILE, TILE), BF),
            pltpu.VMEM((NC * 4, 128), jnp.int32),
            pltpu.SMEM((NC * 4, 128), jnp.int32),
            pltpu.VMEM((NC, 8, 128), jnp.int32),
            pltpu.VMEM((NC, SLOTS, TILE, TILE), BF),
            DMA((7,)), DMA((4,)), DMA((7,)), DMA((7,)), DMA((7,)), DMA((7,)), DMA(()), DMA(()),
            DMA((3,)), DMA((3,)), DMA((2, 4, 4)), DMA((2, 4, 4)),
            DMA((3,)), DMA((3,)), DMA((3, 3)), DMA((3, 3)), DMA((3,)), DMA((3,)),
        ],
        compiler_params=params(8, 0),
    )(owner, source, target, relation, count, tiles, states, weights)


def adjacency_kernel(meta, tiles, adj):
    adj[...] = jnp.zeros_like(adj)

    def slots(c, carry):
        for s in range(SLOTS):
            code = meta[c, s // 2, s % 2]

            @pl.when(code >= 0)
            def _():
                row = pl.ds(pl.multiple_of((code >> 2) * TILE, TILE), TILE)
                column = pl.ds(pl.multiple_of(((s // 2) * 4 + (code & 3)) * TILE, TILE), TILE)
                adj[row, column] += tiles[c, s]

        return carry

    lax.fori_loop(0, NC, slots, 0)


def adjacency(meta, tiles):
    return pl.pallas_call(
        adjacency_kernel,
        out_shape=jax.ShapeDtypeStruct((NY * REL * TILE, 16 * TILE), BF),
        in_specs=[SM, VM],
        out_specs=VM,
        compiler_params=params(6),
    )(meta, tiles)


def main_kernel(
    adj, xp, weights, states, cotangent,
    layer_o, own_o, v_buf, wa, wb,
    tq, tc_buf, ty_src, ty_buf, tg, m_own, m_src, m_buf, my_src, my_buf, slope_s, zs, gw,
    xw_src, xw_buf, zw_src, zw_buf, aw_buf, wb_src, g_in, g_src, g_buf, gx_src, gx_buf, v_src,
    tc_s, tc_r, ty_s, ty_r, mc_s, mc_r, my_s, my_r, s_s, s_r, f_s, f_r,
    xw_s, xw_r, zw_s, zw_r, aw_s, aw_r, wa_s, wa_r, wb_s, wb_r, g_s, g_r, gx_s, gx_r, v_s, v_r,
):
    over_rows = (((0,), (0,)), ((), ()))
    over_columns = (((1,), (1,)), ((), ()))
    z, x, y, p = place()
    core = (z, x, y, 1 - p)
    shifts = (2, 1, 3)
    ys = [(z, x, (y + i) % NY, p) for i in shifts]
    senders = [(y + NY - i) % NY for i in shifts]
    xs = x_peers(z, x, y, p)
    xo = [(q[0], q[1], q[2], 1 - p) for q in xs]
    around = z_peers(z, x, y, p, (4, 3, 5, 2, 6, 1, 7))
    up, down = around[5], around[6]
    target, is_self = swap_of(z, x, y, p)
    arrived = greet([core] + ys + xs + xo + around, (target, is_self))
    c = y * 2 + p
    share = pl.ds(pl.multiple_of(c * ROWS, ROWS), ROWS)

    def half(v, mine):
        low, high = v[:ROWS], v[ROWS:]
        return jnp.where(p == (0 if mine else 1), low, high)

    order = [q[2] for q in ys] + [y]
    m_copies, t_copies, my_copies = [], [], []

    def messages_on(n):
        m_copies[n].wait_recv()
        t = order[n]
        my_src[n] = (m_own[t] + m_buf[t].astype(F32)).astype(BF)
        a = send(my_src.at[n], my_buf.at[n], my_s.at[n], my_r.at[n], *ys[n])
        a.start()
        my_copies.append(a)

    for n, t in enumerate(order):
        rows = pl.ds(pl.multiple_of(t * D, D), D)
        tt = jnp.dot(adj[rows, :], xp[...], preferred_element_type=F32).astype(BF)
        m = jnp.zeros((TILE, D), F32)
        for r in range(REL):
            part = tt[r * TILE : (r + 1) * TILE]
            m = m + jnp.dot(part, weights[r], preferred_element_type=F32)
            for q in range(NY):
                tq[r // 2, t, q, r % 2] = part[:, q * TILE : (q + 1) * TILE]
        m_own[t] = half(m, True)
        m_src[t] = half(m, False).astype(BF)
        if n == 0:
            arrived()
        a = send(m_src.at[t], m_buf.at[t], mc_s.at[n], mc_r.at[n], *core)
        a.start()
        m_copies.append(a)
        if n > 0:
            messages_on(n - 1)
        a = send(tq.at[1 - p, t], tc_buf.at[t], tc_s.at[n], tc_r.at[n], *core)
        a.start()
        t_copies.append(a)

    ty_copies = {}

    def transforms_on(n):
        t = order[n]
        t_copies[n].wait_recv()
        for j, q in enumerate(ys):
            yi = q[2]
            ty_src[j, t] = (tq[p, t, yi].astype(F32) + tc_buf[t, yi].astype(F32)).astype(BF)
            a = send(ty_src.at[j, t], ty_buf.at[j, t], ty_s.at[j, n], ty_r.at[j, n], *q)
            a.start()
            ty_copies[j, n] = a

    transforms_on(0)

    w_self = weights[REL]
    pre = jnp.dot(states[share, :], w_self, preferred_element_type=F32)
    m_copies[3].wait_recv()
    pre = pre + m_own[y] + m_buf[y].astype(F32)
    for n, a in enumerate(my_copies):
        a.wait_recv()
        pre = pre + my_buf[n].astype(F32)
    sigma = jax.nn.sigmoid(pre)
    slope = (cotangent[share, :].astype(F32) * (sigma * (1.0 + pre * (1.0 - sigma)))).astype(BF)
    slope_s[c] = slope
    mine = slope_s.at[c]
    s_copies = []
    for i, q in enumerate(ys + [core]):
        a = send(mine, mine, s_s.at[i], s_r.at[i], *q)
        a.start()
        s_copies.append(a)
    for n in (1, 2, 3):
        transforms_on(n)
    layer_o[...] = pre * sigma
    own_o[...] = lax.dot_general(slope, w_self, over_columns, preferred_element_type=F32)
    f_copies = []
    for i in (1, 2, 0):
        s_copies[i].wait_recv()
        ref = slope_s.at[senders[i] * 2 + p]
        a = send(ref, ref, f_s.at[i], f_r.at[i], *core)
        a.start()
        f_copies.append(a)
    s_copies[3].wait_recv()
    for a in f_copies:
        a.wait_recv()

    whole = slope_s[...].reshape(D, D)
    for r in range(REL):
        part = lax.dot_general(whole, weights[r], over_columns, preferred_element_type=F32)
        part = part.astype(BF)
        for t in range(NY):
            zs[t * D + r * TILE : t * D + (r + 1) * TILE, :] = part[t * TILE : (t + 1) * TILE]

    def gradients(k):
        columns = pl.ds(pl.multiple_of(k * D, D), D)
        part = lax.dot_general(adj[:, columns], zs[...], over_rows, preferred_element_type=F32)
        part = part.astype(BF)
        for b in range(4):
            for h in range(2):
                row = b * TILE + h * ROWS
                g_in[2 * k + h, b] = part[row : row + ROWS]

    g_copies = {}
    hops = {(d, i): 4 if (i < 2) == (d == 0) else 3 for d in range(2) for i in range(NX)}

    def chain(s):
        for i in range(NX):
            xi = (x + i) % NX
            for d, q in ((0, up), (1, down)):
                left = hops[d, i] - s
                if left <= 0:
                    continue
                zd = (z + left) % NZ if d == 0 else (z - left + NZ) % NZ
                if s == 0:
                    src = g_in.at[zd, xi]
                else:
                    g_copies[d, s - 1, i].wait_recv()
                    g_src[d, s - 1, i] = (
                        g_in[zd, xi].astype(F32) + g_buf[d, s - 1, i].astype(F32)
                    ).astype(BF)
                    src = g_src.at[d, s - 1, i]
                a = send(src, g_buf.at[d, s, i], g_s.at[d, s, i], g_r.at[d, s, i], *q)
                a.start()
                g_copies[d, s, i] = a

    pair = z // 2
    odd = 2 * (z % 2)
    gradients((pair + 2) % 4)
    gradients((pair + 1 + odd) % 4)
    chain(0)
    gradients((pair + 3 + odd) % 4)
    chain(1)
    gradients(pair)

    for a in ty_copies.values():
        a.wait_recv()
    for t in range(NY):
        total = tq[p, t, y].astype(F32) + tc_buf[t, y].astype(F32)
        for j in range(3):
            total = total + ty_buf[j, t].astype(F32)
        for r in range(2):
            tg[r, t * TILE : (t + 1) * TILE, :] = total[r].astype(BF)
    parts = [
        lax.dot_general(tg[r], whole, over_rows, preferred_element_type=F32) for r in range(2)
    ]
    columns = pl.ds(pl.multiple_of(y * TILE, TILE), TILE)
    self_part = lax.dot_general(states[:, columns], whole, over_rows, preferred_element_type=F32)
    rows_of = [half(v, True) for v in parts] + [half(self_part, True)] + [half(v, False) for v in parts]
    for m, v in enumerate(rows_of):
        for q in range(NX):
            gw[q, m * ROWS : (m + 1) * ROWS, :] = v[:, q * WC : (q + 1) * WC]
    xw_copies = []
    for i in range(3):
        xw_src[i] = gw[xs[i][1]].astype(BF)
        a = send(xw_src.at[i], xw_buf.at[i], xw_s.at[i], xw_r.at[i], *xs[i])
        a.start()
        xw_copies.append(a)
    chain(2)
    total = gw[x]
    for i, a in enumerate(xw_copies):
        a.wait_recv()
        total = total + xw_buf[i].astype(F32)
    zw_src[...] = total.reshape(NZ, WROWS // NZ, WC)
    zw_copies = []
    for i, q in enumerate(around):
        a = send(zw_src.at[q[0]], zw_buf.at[i], zw_s.at[i], zw_r.at[i], *q)
        a.start()
        zw_copies.append(a)
    chain(3)
    total = zw_src[z]
    for i, a in enumerate(zw_copies):
        a.wait_recv()
        total = total + zw_buf[i]
    aw_buf[z] = total
    aw_copies = []
    for i, q in enumerate(around):
        a = send(aw_buf.at[z], aw_buf.at[z], aw_s.at[i], aw_r.at[i], *q)
        a.start()
        aw_copies.append(a)

    gx_copies = []
    own = None
    for i in (1, 2, 3, 0):
        xi = (x + i) % NX
        part = g_in[z, xi].astype(F32)
        for d in range(2):
            last = hops[d, i] - 1
            g_copies[d, last, i].wait_recv()
            part = part + g_buf[d, last, i].astype(F32)
        if i:
            gx_src[i - 1] = part.astype(BF)
            a = send(gx_src.at[i - 1], gx_buf.at[i - 1], gx_s.at[i - 1], gx_r.at[i - 1], *xs[i - 1])
            a.start()
            gx_copies.append(a)
        else:
            own = part

    for a in aw_copies:
        a.wait_recv()
    done = aw_buf[...].reshape(WROWS, WC).astype(BF)
    wa[x] = done[: 3 * ROWS]
    wb_src[...] = done[3 * ROWS :]
    w_copies = []
    for i, q in enumerate(xs):
        w_copies.append(send(wa.at[x], wa.at[x], wa_s.at[i], wa_r.at[i], *q))
    for i, q in enumerate(xo + [core]):
        w_copies.append(send(wb_src, wb.at[x], wb_s.at[i], wb_r.at[i], *q))
    for a in w_copies:
        a.start()

    for i, a in enumerate(gx_copies):
        a.wait_recv()
        own = own + gx_buf[i].astype(F32)
    v_src[...] = own.astype(BF)

    @pl.when(jnp.logical_not(is_self))
    def _():
        a = send(v_src, v_buf, v_s, v_r, *target)
        a.start()
        a.wait()

    @pl.when(is_self)
    def _():
        v_buf[...] = v_src[...]

    for a in w_copies:
        a.wait()
    for a in m_copies + t_copies + my_copies + s_copies + f_copies:
        a.wait_send()
    for a in xw_copies + zw_copies + aw_copies + gx_copies:
        a.wait_send()
    for a in list(ty_copies.values()) + list(g_copies.values()):
        a.wait_send()


def main(adj, xp, weights, states, cotangent):
    return pl.pallas_call(
        main_kernel,
        out_shape=(
            jax.ShapeDtypeStruct((ROWS, D), F32),
            jax.ShapeDtypeStruct((ROWS, D), F32),
            jax.ShapeDtypeStruct((ROWS, D), BF),
            jax.ShapeDtypeStruct((NX, 3 * ROWS, WC), BF),
            jax.ShapeDtypeStruct((NX, 2 * ROWS, WC), BF),
        ),
        in_specs=[VM] * 5,
        out_specs=(VM,) * 5,
        scratch_shapes=[
            pltpu.VMEM((2, NY, NY, 2, TILE, TILE), BF),
            pltpu.VMEM((NY, NY, 2, TILE, TILE), BF),
            pltpu.VMEM((3, NY, 2, TILE, TILE), BF),
            pltpu.VMEM((3, NY, 2, TILE, TILE), BF),
            pltpu.VMEM((2, D, TILE), BF),
            pltpu.VMEM((NY, ROWS, D), F32),
            pltpu.VMEM((NY, ROWS, D), BF),
            pltpu.VMEM((NY, ROWS, D), BF),
            pltpu.VMEM((3, ROWS, D), BF),
            pltpu.VMEM((3, ROWS, D), BF),
            pltpu.VMEM((NC, ROWS, D), BF),
            pltpu.VMEM((NY * D, D), BF),
            pltpu.VMEM((NX, WROWS, WC), F32),
            pltpu.VMEM((3, WROWS, WC), BF),
            pltpu.VMEM((3, WROWS, WC), BF),
            pltpu.VMEM((NZ, WROWS // NZ, WC), F32),
            pltpu.VMEM((7, WROWS // NZ, WC), F32),
            pltpu.VMEM((NZ, WROWS // NZ, WC), F32),
            pltpu.VMEM((2 * ROWS, WC), BF),
            pltpu.VMEM((NZ, NX, ROWS, D), BF),
            pltpu.VMEM((2, 3, NX, ROWS, D), BF),
            pltpu.VMEM((2, 4, NX, ROWS, D), BF),
            pltpu.VMEM((3, ROWS, D), BF),
            pltpu.VMEM((3, ROWS, D), BF),
            pltpu.VMEM((ROWS, D), BF),
            DMA((4,)), DMA((4,)), DMA((3, 4)), DMA((3, 4)), DMA((4,)), DMA((4,)), DMA((3,)), DMA((3,)),
            DMA((4,)), DMA((4,)), DMA((3,)), DMA((3,)),
            DMA((3,)), DMA((3,)), DMA((7,)), DMA((7,)), DMA((7,)), DMA((7,)), DMA((3,)), DMA((3,)),
            DMA((4,)), DMA((4,)), DMA((2, 4, 4)), DMA((2, 4, 4)), DMA((3,)), DMA((3,)), DMA(()), DMA(()),
        ],
        compiler_params=params(32, 1),
    )(adj, xp, weights, states, cotangent)


def close_kernel(layer, own, v, wa, wb, layer_o, g_o, w_o):
    p = lax.axis_index("replica")
    layer_o[...] = layer[...]
    g_o[...] = own[...] + v[...].astype(F32)
    for q in range(NX):
        columns = slice(q * WC, (q + 1) * WC)
        for m in range(2):
            a = wa[q, m * ROWS : (m + 1) * ROWS, :].astype(F32)
            b = wb[q, m * ROWS : (m + 1) * ROWS, :].astype(F32)
            w_o[m, :, columns] = jnp.where(p == 0, a, b)
            w_o[2 + m, :, columns] = jnp.where(p == 0, b, a)
        w_o[REL, :, columns] = wa[q, 2 * ROWS :, :].astype(F32)


def close(layer, own, v, wa, wb):
    return pl.pallas_call(
        close_kernel,
        out_shape=(
            jax.ShapeDtypeStruct((ROWS, D), F32),
            jax.ShapeDtypeStruct((ROWS, D), F32),
            jax.ShapeDtypeStruct((REL + 1, ROWS, D), F32),
        ),
        in_specs=[VM] * 5,
        out_specs=(VM, VM, VM),
        compiler_params=params(8),
    )(layer, own, v, wa, wb)


def shards(
    states,
    weights,
    edge_tiles,
    edge_owner,
    edge_source,
    edge_target,
    edge_relation,
    edge_count,
    cotangent,
):
    groups = edge_owner.shape[0]
    owner = edge_owner.reshape(groups, EB)
    source = edge_source.reshape(groups, EB)
    target = edge_target.reshape(groups, EB)
    relation = edge_relation.reshape(groups, EB)
    count = edge_count.reshape(1, groups)
    tiles = edge_tiles.reshape(EB, TILE, TILE)
    tiles, meta, xp, full = deal(owner, source, target, relation, count, tiles, states, weights)
    adj = adjacency(meta, tiles)
    layer, own, v, wa, wb = main(adj, xp.reshape(-1, D), full, states, cotangent)
    return close(layer, own, v, wa, wb)


def solution(mesh):
    return jax.shard_map(
        shards,
        mesh=mesh,
        in_specs=(
            P("graph", None),
            P(None, "fsdp", None),
            P("graph", "fsdp", "replica", None, None, None),
            P(None, "fsdp", "replica", None),
            P(None, "fsdp", "replica", None),
            P(None, "fsdp", "replica", None),
            P(None, "fsdp", "replica", None),
            P(None, "fsdp", "replica"),
            P("graph", None),
        ),
        out_specs=(
            P(("graph", "fsdp", "replica"), None),
            P(("graph", "fsdp", "replica"), None),
            P(None, ("fsdp", "replica"), None),
        ),
        check_vma=False,
    )
```

time: 140 us -> 117 us (0.84)
  Pallas kernels: 131 us -> 108 us
    pallas_call x5 -> x2, Pallas kernels: 90.7 us -> 68.2 us  [the longest x1 65.6 us: main(): pl.pallas_call(main_kernel, out_shape=(jax.ShapeDtypeStruct((ROWS, D), F3...]
where the time goes in v3:
time: 117 us; the launch traced here: 116 us
  Pallas kernels  108 us (92%)
  local copies, waits for them, and re-layouts  7.07 us (6%)
    pallas_call x1, Pallas kernels, main(): pl.pallas_call(main_kernel, out_shape=(jax.ShapeDtypeStruct((ROWS, D), F3...  65.6 us
    pallas_call x1, Pallas kernels, deal(): pl.pallas_call(deal_kernel, out_shape=(jax.ShapeDtypeStruct((NC, SLOTS, T...  39.1 us
    unnamed x20, local copies, waits for them, and re-layouts  7.07 us
    pallas_call x1, Pallas kernels, adjacency(): pl.pallas_call(adjacency_kernel, out_shape=jax.ShapeDtypeStruct((NY * REL...  2.61 us

profile of v3, /device:TPU:24, one launch (start us, length us, event | category | flops | bytes accessed | tf_op | source)
XLA Modules:
  0.0 116.0 jit_solution(14761819388155556294)
XLA Ops:
  0.6 0.0 copy-start
  0.6 1.0 copy-done
  1.7 0.0 copy-start.2
  1.7 1.4 %copy-done.2 = bf16[1,1,1,48,128,128]{5,4,3,2,1,0:T(8,128)(2,1)S(1)} copy-done((bf16[1,1,1,48,128,128]{5,4,3,2,1,0:T(8,128)(2,1)S(1)}, bf16[1,1,1,48,128,128]{5,4,3,2,1,0:T(8,128)(2,1)}, u32[]{:S(2)}) %copy-start.2) | copy-done | bytes 1572888
  3.1 0.0 copy-start.3
  3.1 1.1 copy-done.3
  4.2 0.0 copy-start.5
  4.2 0.7 copy-done.5
  4.9 0.0 copy-start.6
  4.9 0.7 copy-done.6
  5.6 0.0 copy-start.7
  5.6 0.7 copy-done.7
  6.3 0.0 copy-start.8
  6.3 0.7 copy-done.8
  7.0 0.0 copy-start.9
  7.0 0.7 copy-done.9
  7.7 39.1 %shard_map.112 = (bf16[8,8,128,128]{3,2,1,0:T(8,128)(2,1)S(1)}, s32[8,8,128]{2,1,0:T(8,128)S(1)}, bf16[8,4,64,512]{3,2,1,0:T(8,128)(2,1)S(1)}, bf16[5,512,512]{2,1,0:T(8,128)(2,1)S(1)}) custom-call(s32[32,48]{1,0:T(8,128)S(1)} %bitcast.9, s32[32,48]{1,0:T(8,128)S(1)} %bitcast.10, s32[32,48]{1,0:T(8,128)S(1)} %bitcast.11, s32[32,48]{1,0:T(8,128)S(1)} %bitcast.12, ...), custom_call_target="tpu_custom_call" | custom-call | tf_op jit(solution)/shard_map/pallas_call | solution.py:249
  46.8 0.0 copy-start.1
  46.8 0.0 copy-start.4
  46.8 2.6 %shard_map.113.adj = bf16[2048,2048]{1,0:T(8,128)(2,1)S(1)} custom-call(s32[8,8,128]{2,1,0:T(8,128)S(1)} %get-tuple-element.12.meta, bf16[8,8,128,128]{3,2,1,0:T(8,128)(2,1)S(1)} %get-tuple-element.13.tiles), custom_call_target="tpu_custom_call" | custom-call | tf_op jit(solution)/shard_map/pallas_call | solution.py:294
  49.4 0.0 copy-done.1
  49.4 0.0 copy-done.4
  49.4 65.6 %shard_map.114 = (f32[64,512]{1,0:T(8,128)S(1)}, f32[64,512]{1,0:T(8,128)S(1)}, bf16[64,512]{1,0:T(8,128)(2,1)S(1)}, bf16[4,192,128]{2,1,0:T(8,128)(2,1)S(1)}, bf16[4,128,128]{2,1,0:T(8,128)(2,1)S(1)}) custom-call(bf16[2048,2048]{1,0:T(8,128)(2,1)S(1)} %shard_map.113.adj, bf16[2048,512]{1,0:T(8,128)(2,1)S(1)} %bitcast.7, ...), custom_call_target="tpu_custom_call" | custom-call | tf_op jit(solution)/shard_map/pallas_call | solution.py:559
  115.1 1.0 shard_map.115
Async XLA Ops:
  0.6 1.0 copy-start
  1.7 1.4 %copy-start.2 = (bf16[1,1,1,48,128,128]{5,4,3,2,1,0:T(8,128)(2,1)S(1)}, bf16[1,1,1,48,128,128]{5,4,3,2,1,0:T(8,128)(2,1)}, u32[]{:S(2)}) copy-start(bf16[1,1,1,48,128,128]{5,4,3,2,1,0:T(8,128)(2,1)} %param.11) | copy-start | bytes 4718596
  3.1 1.1 copy-start.3
  4.2 0.7 copy-start.5
  4.9 0.7 copy-start.6
  5.6 0.7 copy-start.7
  6.3 0.7 copy-start.8
  7.0 0.7 copy-start.9
  46.8 2.6 %copy-start.1 = (bf16[512,512]{1,0:T(8,128)(2,1)S(1)}, bf16[512,512]{1,0:T(8,128)(2,1)}, u32[]{:S(2)}) copy-start(bf16[512,512]{1,0:T(8,128)(2,1)} %states.3) | copy-start | bytes 1572868
  46.8 2.6 %copy-start.4 = (bf16[512,512]{1,0:T(8,128)(2,1)S(1)}, bf16[512,512]{1,0:T(8,128)(2,1)}, u32[]{:S(2)}) copy-start(bf16[512,512]{1,0:T(8,128)(2,1)} %cotangent.1) | copy-start | bytes 1572868

commit v4 on v3

--- a/solution.py
+++ b/solution.py
@@ -16,6 +16,9 @@
 SLOTS = 8
 ROWS = 64
 WROWS = 320
+ZROWS = 48
+HA = 32
+HB = ROWS - HA
 WC = 128
 BF = jnp.bfloat16
 F32 = jnp.float32
@@ -23,7 +26,7 @@
 ANY = pl.BlockSpec(memory_space=pl.ANY)
 VM = pl.BlockSpec(memory_space=pltpu.VMEM)
 SM = pl.BlockSpec(memory_space=pltpu.SMEM)
-HB = pl.BlockSpec(memory_space=pltpu.HBM)
+IN_HBM = pl.BlockSpec(memory_space=pltpu.HBM)
 DMA = pltpu.SemaphoreType.DMA
 
 
@@ -99,7 +102,6 @@
     xs = x_peers(z, x, y, p)
     up, down = z_peers(z, x, y, p)
     target, is_self = swap_of(z, x, y, p)
-    arrived = greet(peers + xs + [up, down], (target, is_self))
     loads = [
         pltpu.make_async_copy(h, edges.at[i], e_sems.at[i])
         for i, h in enumerate((owner, source, target_h, relation))
@@ -109,6 +111,7 @@
         a.start()
     load_tiles = pltpu.make_async_copy(tiles, tiles_v, e_sems.at[5])
     load_tiles.start()
+    arrived = greet(peers + xs + [up, down], (target, is_self))
     c = y * 2 + p
     piece = states.at[pl.ds(pl.multiple_of((p * NY + y) * ROWS, ROWS), ROWS)]
 
@@ -172,8 +175,26 @@
 
         lax.fori_loop(0, SLOTS, one, 0)
 
+    x_copies = [
+        send(xp.at[z, x], xp.at[z, x], x_send.at[i], x_recv.at[i], *q) for i, q in enumerate(xs)
+    ]
+
+    def x_phase():
+        @pl.when(jnp.logical_not(is_self))
+        def _():
+            send(piece, xp.at[z, x], v_send, v_recv, *target).wait()
+
+        @pl.when(is_self)
+        def _():
+            pltpu.make_async_copy(piece, xp.at[z, x], own_sems.at[0]).wait()
+
+        for a in x_copies:
+            a.start()
+
     tile_copies = []
     for i, q in enumerate(peers):
+        if i == 3:
+            x_phase()
         cq = q[2] * 2 + q[3]
         put(cq)
         a = send(packed.at[cq], tiles_o.at[c], t_send.at[i], t_recv.at[i], *q)
@@ -189,20 +210,6 @@
     for a in own_copies:
         a.start()
     own_copies.append(own_w)
-
-    @pl.when(jnp.logical_not(is_self))
-    def _():
-        send(piece, xp.at[z, x], v_send, v_recv, *target).wait()
-
-    @pl.when(is_self)
-    def _():
-        pltpu.make_async_copy(piece, xp.at[z, x], own_sems.at[0]).wait()
-
-    x_copies = [
-        send(xp.at[z, x], xp.at[z, x], x_send.at[i], x_recv.at[i], *q) for i, q in enumerate(xs)
-    ]
-    for a in x_copies:
-        a.start()
 
     wx_copies = []
     wc_copies = []
@@ -254,7 +261,7 @@
             jax.ShapeDtypeStruct((NZ, NX, ROWS, D), BF),
             jax.ShapeDtypeStruct((REL + 1, D, D), BF),
         ),
-        in_specs=[HB] * 8,
+        in_specs=[IN_HBM] * 8,
         out_specs=(ANY,) * 4,
         scratch_shapes=[
             pltpu.VMEM((4, NZ * NX, EB), jnp.int32),
@@ -304,9 +311,11 @@
     adj, xp, weights, states, cotangent,
     layer_o, own_o, v_buf, wa, wb,
     tq, tc_buf, ty_src, ty_buf, tg, m_own, m_src, m_buf, my_src, my_buf, slope_s, zs, gw,
-    xw_src, xw_buf, zw_src, zw_buf, aw_buf, wb_src, g_in, g_src, g_buf, gx_src, gx_buf, v_src,
+    xw_src, xw_buf, zw_src, zw_buf, aw_buf, wb_src, g_in, g_src, g_buf, gx_src, gx_buf,
+    bx_buf, b_src, b_buf, v_src,
     tc_s, tc_r, ty_s, ty_r, mc_s, mc_r, my_s, my_r, s_s, s_r, f_s, f_r,
-    xw_s, xw_r, zw_s, zw_r, aw_s, aw_r, wa_s, wa_r, wb_s, wb_r, g_s, g_r, gx_s, gx_r, v_s, v_r,
+    xw_s, xw_r, zw_s, zw_r, aw_s, aw_r, wa_s, wa_r, wb_s, wb_r, g_s, g_r, gx_s, gx_r,
+    bx_s, bx_r, b_s, b_r, v_s, v_r,
 ):
     over_rows = (((0,), (0,)), ((), ()))
     over_columns = (((1,), (1,)), ((), ()))
@@ -339,6 +348,18 @@
         a.start()
         my_copies.append(a)
 
+    ty_copies = {}
+
+    def transforms_on(n):
+        t = order[n]
+        t_copies[n].wait_recv()
+        for j, q in enumerate(ys):
+            yi = q[2]
+            ty_src[j, t] = (tq[p, t, yi].astype(F32) + tc_buf[t, yi].astype(F32)).astype(BF)
+            a = send(ty_src.at[j, t], ty_buf.at[j, t], ty_s.at[j, n], ty_r.at[j, n], *q)
+            a.start()
+            ty_copies[j, n] = a
+
     for n, t in enumerate(order):
         rows = pl.ds(pl.multiple_of(t * D, D), D)
         tt = jnp.dot(adj[rows, :], xp[...], preferred_element_type=F32).astype(BF)
@@ -357,23 +378,13 @@
         m_copies.append(a)
         if n > 0:
             messages_on(n - 1)
+        if n == 1:
+            transforms_on(0)
         a = send(tq.at[1 - p, t], tc_buf.at[t], tc_s.at[n], tc_r.at[n], *core)
         a.start()
         t_copies.append(a)
 
-    ty_copies = {}
-
-    def transforms_on(n):
-        t = order[n]
-        t_copies[n].wait_recv()
-        for j, q in enumerate(ys):
-            yi = q[2]
-            ty_src[j, t] = (tq[p, t, yi].astype(F32) + tc_buf[t, yi].astype(F32)).astype(BF)
-            a = send(ty_src.at[j, t], ty_buf.at[j, t], ty_s.at[j, n], ty_r.at[j, n], *q)
-            a.start()
-            ty_copies[j, n] = a
-
-    transforms_on(0)
+    transforms_on(1)
 
     w_self = weights[REL]
     pre = jnp.dot(states[share, :], w_self, preferred_element_type=F32)
@@ -391,7 +402,7 @@
         a = send(mine, mine, s_s.at[i], s_r.at[i], *q)
         a.start()
         s_copies.append(a)
-    for n in (1, 2, 3):
+    for n in (2, 3):
         transforms_on(n)
     layer_o[...] = pre * sigma
     own_o[...] = lax.dot_general(slope, w_self, over_columns, preferred_element_type=F32)
@@ -425,6 +436,9 @@
     g_copies = {}
     hops = {(d, i): 4 if (i < 2) == (d == 0) else 3 for d in range(2) for i in range(NX)}
 
+    def toward(d, left):
+        return (z + left) % NZ if d == 0 else (z - left + NZ) % NZ
+
     def chain(s):
         for i in range(NX):
             xi = (x + i) % NX
@@ -432,27 +446,72 @@
                 left = hops[d, i] - s
                 if left <= 0:
                     continue
-                zd = (z + left) % NZ if d == 0 else (z - left + NZ) % NZ
+                zd = toward(d, left)
                 if s == 0:
-                    src = g_in.at[zd, xi]
+                    src = g_in.at[zd, xi, pl.ds(0, HA)]
                 else:
                     g_copies[d, s - 1, i].wait_recv()
                     g_src[d, s - 1, i] = (
-                        g_in[zd, xi].astype(F32) + g_buf[d, s - 1, i].astype(F32)
+                        g_in[zd, xi, :HA].astype(F32) + g_buf[d, s - 1, i].astype(F32)
                     ).astype(BF)
                     src = g_src.at[d, s - 1, i]
                 a = send(src, g_buf.at[d, s, i], g_s.at[d, s, i], g_r.at[d, s, i], *q)
                 a.start()
                 g_copies[d, s, i] = a
 
+    bx_copies = {}
+    b_copies = {}
+
+    def across(n, k):
+        two = pl.ds(2 * k, 2)
+        for j, q in enumerate(xs):
+            a = send(
+                g_in.at[two, q[1], pl.ds(HA, HB)], bx_buf.at[j, two], bx_s.at[j, n], bx_r.at[j, n], *q
+            )
+            a.start()
+            bx_copies[j, n] = a
+
+    def across_wait(n):
+        for j in range(3):
+            bx_copies[j, n].wait_recv()
+
+    def x_sum(zd, h):
+        columns = slice(h * 256, (h + 1) * 256)
+        total = g_in[zd, x, HA:, columns].astype(F32)
+        for j in range(3):
+            total = total + bx_buf[j, zd, :, columns].astype(F32)
+        return total
+
+    def second_chain(s):
+        for h in range(2):
+            for d, q in ((0, up), (1, down)):
+                left = (4 if h == d else 3) - s
+                if left <= 0:
+                    continue
+                total = x_sum(toward(d, left), h)
+                if s > 0:
+                    b_copies[d, s - 1, h].wait_recv()
+                    total = total + b_buf[d, s - 1, h].astype(F32)
+                b_src[d, s, h] = total.astype(BF)
+                a = send(b_src.at[d, s, h], b_buf.at[d, s, h], b_s.at[d, s, h], b_r.at[d, s, h], *q)
+                a.start()
+                b_copies[d, s, h] = a
+
     pair = z // 2
     odd = 2 * (z % 2)
-    gradients((pair + 2) % 4)
-    gradients((pair + 1 + odd) % 4)
+    near = ((pair + 2) % 4, (pair + 1 + odd) % 4, (pair + 3 + odd) % 4, pair)
+    for n in (0, 1):
+        gradients(near[n])
+        across(n, near[n])
     chain(0)
-    gradients((pair + 3 + odd) % 4)
+    gradients(near[2])
+    across(2, near[2])
     chain(1)
-    gradients(pair)
+    gradients(near[3])
+    across(3, near[3])
+    across_wait(0)
+    across_wait(1)
+    second_chain(0)
 
     for a in ty_copies.values():
         a.wait_recv()
@@ -478,33 +537,41 @@
         a.start()
         xw_copies.append(a)
     chain(2)
+    across_wait(2)
+    second_chain(1)
     total = gw[x]
     for i, a in enumerate(xw_copies):
         a.wait_recv()
         total = total + xw_buf[i].astype(F32)
-    zw_src[...] = total.reshape(NZ, WROWS // NZ, WC)
+    padding = jnp.zeros((NZ, ZROWS - WROWS // NZ, WC), F32)
+    zw_src[...] = jnp.concatenate(
+        [total.reshape(NZ, WROWS // NZ, WC), padding], axis=1
+    ).astype(BF)
     zw_copies = []
     for i, q in enumerate(around):
         a = send(zw_src.at[q[0]], zw_buf.at[i], zw_s.at[i], zw_r.at[i], *q)
         a.start()
         zw_copies.append(a)
     chain(3)
-    total = zw_src[z]
+    across_wait(3)
+    second_chain(2)
+    total = zw_src[z].astype(F32)
     for i, a in enumerate(zw_copies):
         a.wait_recv()
-        total = total + zw_buf[i]
-    aw_buf[z] = total
+        total = total + zw_buf[i].astype(F32)
+    aw_buf[z] = total.astype(BF)
     aw_copies = []
     for i, q in enumerate(around):
         a = send(aw_buf.at[z], aw_buf.at[z], aw_s.at[i], aw_r.at[i], *q)
         a.start()
         aw_copies.append(a)
 
+    second_chain(3)
     gx_copies = []
     own = None
     for i in (1, 2, 3, 0):
         xi = (x + i) % NX
-        part = g_in[z, xi].astype(F32)
+        part = g_in[z, xi, :HA].astype(F32)
         for d in range(2):
             last = hops[d, i] - 1
             g_copies[d, last, i].wait_recv()
@@ -519,7 +586,7 @@
 
     for a in aw_copies:
         a.wait_recv()
-    done = aw_buf[...].reshape(WROWS, WC).astype(BF)
+    done = aw_buf[...].astype(F32)[:, : WROWS // NZ].reshape(WROWS, WC).astype(BF)
     wa[x] = done[: 3 * ROWS]
     wb_src[...] = done[3 * ROWS :]
     w_copies = []
@@ -533,7 +600,14 @@
     for i, a in enumerate(gx_copies):
         a.wait_recv()
         own = own + gx_buf[i].astype(F32)
-    v_src[...] = own.astype(BF)
+    v_src[:HA] = own.astype(BF)
+    for h in range(2):
+        part = x_sum(z, h)
+        for d in range(2):
+            last = (4 if h == d else 3) - 1
+            b_copies[d, last, h].wait_recv()
+            part = part + b_buf[d, last, h].astype(F32)
+        v_src[HA:, h * 256 : (h + 1) * 256] = part.astype(BF)
 
     @pl.when(jnp.logical_not(is_self))
     def _():
@@ -551,8 +625,9 @@
         a.wait_send()
     for a in xw_copies + zw_copies + aw_copies + gx_copies:
         a.wait_send()
-    for a in list(ty_copies.values()) + list(g_copies.values()):
-        a.wait_send()
+    for some in (ty_copies, g_copies, bx_copies, b_copies):
+        for a in some.values():
+            a.wait_send()
 
 
 def main(adj, xp, weights, states, cotangent):
@@ -583,20 +658,24 @@
             pltpu.VMEM((NX, WROWS, WC), F32),
             pltpu.VMEM((3, WROWS, WC), BF),
             pltpu.VMEM((3, WROWS, WC), BF),
-            pltpu.VMEM((NZ, WROWS // NZ, WC), F32),
-            pltpu.VMEM((7, WROWS // NZ, WC), F32),
-            pltpu.VMEM((NZ, WROWS // NZ, WC), F32),
+            pltpu.VMEM((NZ, ZROWS, WC), BF),
+            pltpu.VMEM((7, ZROWS, WC), BF),
+            pltpu.VMEM((NZ, ZROWS, WC), BF),
             pltpu.VMEM((2 * ROWS, WC), BF),
             pltpu.VMEM((NZ, NX, ROWS, D), BF),
-            pltpu.VMEM((2, 3, NX, ROWS, D), BF),
-            pltpu.VMEM((2, 4, NX, ROWS, D), BF),
-            pltpu.VMEM((3, ROWS, D), BF),
-            pltpu.VMEM((3, ROWS, D), BF),
+            pltpu.VMEM((2, 3, NX, HA, D), BF),
+            pltpu.VMEM((2, 4, NX, HA, D), BF),
+            pltpu.VMEM((3, HA, D), BF),
+            pltpu.VMEM((3, HA, D), BF),
+            pltpu.VMEM((3, NZ, HB, D), BF),
+            pltpu.VMEM((2, 4, 2, HB, 256), BF),
+            pltpu.VMEM((2, 4, 2, HB, 256), BF),
             pltpu.VMEM((ROWS, D), BF),
             DMA((4,)), DMA((4,)), DMA((3, 4)), DMA((3, 4)), DMA((4,)), DMA((4,)), DMA((3,)), DMA((3,)),
             DMA((4,)), DMA((4,)), DMA((3,)), DMA((3,)),
             DMA((3,)), DMA((3,)), DMA((7,)), DMA((7,)), DMA((7,)), DMA((7,)), DMA((3,)), DMA((3,)),
-            DMA((4,)), DMA((4,)), DMA((2, 4, 4)), DMA((2, 4, 4)), DMA((3,)), DMA((3,)), DMA(()), DMA(()),
+            DMA((4,)), DMA((4,)), DMA((2, 4, 4)), DMA((2, 4, 4)), DMA((3,)), DMA((3,)),
+            DMA((3, 4)), DMA((3, 4)), DMA((2, 4, 2)), DMA((2, 4, 2)), DMA(()), DMA(()),
         ],
         compiler_params=params(32, 1),
     )(adj, xp, weights, states, cotangent)
@@ -648,7 +727,9 @@
     relation = edge_relation.reshape(groups, EB)
     count = edge_count.reshape(1, groups)
     tiles = edge_tiles.reshape(EB, TILE, TILE)
-    tiles, meta, xp, full = deal(owner, source, target, relation, count, tiles, states, weights)
+    given = (owner, source, target, relation, count, tiles, states, weights)
+    given = (pltpu.with_memory_space_constraint(v, pltpu.HBM) for v in given)
+    tiles, meta, xp, full = deal(*given)
     adj = adjacency(meta, tiles)
     layer, own, v, wa, wb = main(adj, xp.reshape(-1, D), full, states, cotangent)
     return close(layer, own, v, wa, wb)

time: 117 us -> 107 us (0.915)
  local copies, waits for them, and re-layouts: 7.07 us -> 0.01 us
  Pallas kernels: 108 us -> 106 us
    unnamed x20 -> x4, local copies, waits for them, and re-layouts: 7.07 us -> 0.01 us
    pallas_call x1, Pallas kernels: 65.6 us -> 62.8 us  [main(): pl.pallas_call(main_kernel, out_shape=(jax.ShapeDtypeStruct((ROWS, D), F3...]
where the time goes in v4:
time: 107 us
  Pallas kernels  106 us (99%)
    pallas_call x1, Pallas kernels, main(): pl.pallas_call(main_kernel, out_shape=(jax.ShapeDtypeStruct((ROWS, D), F3...  62.8 us
    pallas_call x1, Pallas kernels, deal(): pl.pallas_call(deal_kernel, out_shape=(jax.ShapeDtypeStruct((NC, SLOTS, T...  39.6 us
    pallas_call x1, Pallas kernels, adjacency(): pl.pallas_call(adjacency_kernel, out_shape=jax.ShapeDtypeStruct((NY * REL...  2.59 us

profile of v4, /device:TPU:24, one launch (start us, length us, event | category | flops | bytes accessed | tf_op | source)
XLA Modules:
  0.0 106.7 jit_solution(15662624843671886911)
XLA Ops:
  0.6 39.6 %shard_map.112 = (bf16[8,8,128,128]{3,2,1,0:T(8,128)(2,1)S(1)}, s32[8,8,128]{2,1,0:T(8,128)S(1)}, bf16[8,4,64,512]{3,2,1,0:T(8,128)(2,1)S(1)}, bf16[5,512,512]{2,1,0:T(8,128)(2,1)S(1)}) custom-call(s32[32,48]{1,0:T(8,128)} %bitcast.9, s32[32,48]{1,0:T(8,128)} %bitcast.10, s32[32,48]{1,0:T(8,128)} %bitcast.11, s32[32,48]{1,0:T(8,128)} %bitcast.12, ...), custom_call_target="tpu_custom_call" | custom-call | tf_op jit(solution)/shard_map/pallas_call | solution.py:256
  40.2 0.0 copy-start
  40.2 0.0 copy-start.1
  40.3 2.6 %shard_map.113.adj = bf16[2048,2048]{1,0:T(8,128)(2,1)S(1)} custom-call(s32[8,8,128]{2,1,0:T(8,128)S(1)} %get-tuple-element.12.meta, bf16[8,8,128,128]{3,2,1,0:T(8,128)(2,1)S(1)} %get-tuple-element.13.tiles), custom_call_target="tpu_custom_call" | custom-call | tf_op jit(solution)/shard_map/pallas_call | solution.py:301
  42.9 0.0 copy-done
  42.9 0.0 copy-done.1
  42.9 62.8 %shard_map.114 = (f32[64,512]{1,0:T(8,128)S(1)}, f32[64,512]{1,0:T(8,128)S(1)}, bf16[64,512]{1,0:T(8,128)(2,1)S(1)}, bf16[4,192,128]{2,1,0:T(8,128)(2,1)S(1)}, bf16[4,128,128]{2,1,0:T(8,128)(2,1)S(1)}) custom-call(bf16[2048,2048]{1,0:T(8,128)(2,1)S(1)} %shard_map.113.adj, bf16[2048,512]{1,0:T(8,128)(2,1)S(1)} %bitcast.7, ...), custom_call_target="tpu_custom_call" | custom-call | tf_op jit(solution)/shard_map/pallas_call | solution.py:634
  105.7 1.0 shard_map.115
Async XLA Ops:
  40.2 2.6 %copy-start = (bf16[512,512]{1,0:T(8,128)(2,1)S(1)}, bf16[512,512]{1,0:T(8,128)(2,1)}, u32[]{:S(2)}) copy-start(bf16[512,512]{1,0:T(8,128)(2,1)} %states.3) | copy-start | bytes 1572868
  40.2 2.6 %copy-start.1 = (bf16[512,512]{1,0:T(8,128)(2,1)S(1)}, bf16[512,512]{1,0:T(8,128)(2,1)}, u32[]{:S(2)}) copy-start(bf16[512,512]{1,0:T(8,128)(2,1)} %cotangent.1) | copy-start | bytes 1572868

commit v5 on v4

--- a/solution.py
+++ b/solution.py
@@ -15,9 +15,9 @@
 NC = 8
 SLOTS = 8
 ROWS = 64
-WROWS = 320
-ZROWS = 48
-HA = 32
+PART = (128, 192)
+EIGHTH = (16, 32)
+HA = 48
 HB = ROWS - HA
 WC = 128
 BF = jnp.bfloat16
@@ -91,7 +91,7 @@
 
 
 def deal_kernel(
-    owner, source, target_h, relation, count, tiles, states, weights, tiles_o, meta_o, xp, full,
+    owner, source, target_h, relation, count, tiles, states, weights, tiles_o, meta_o, xp, full, zeros,
     edges, counts, tiles_v, idx_v, idx, meta, packed,
     e_sems, own_sems, t_send, t_recv, m_send, m_recv, v_send, v_recv, x_send, x_recv, z_send, z_recv,
     wy_send, wy_recv, wx_send, wx_recv, wc_send, wc_recv,
@@ -210,6 +210,8 @@
     for a in own_copies:
         a.start()
     own_copies.append(own_w)
+
+    zeros[...] = jnp.zeros_like(zeros)
 
     wx_copies = []
     wc_copies = []
@@ -260,9 +262,10 @@
             jax.ShapeDtypeStruct((NC, 8, 128), jnp.int32),
             jax.ShapeDtypeStruct((NZ, NX, ROWS, D), BF),
             jax.ShapeDtypeStruct((REL + 1, D, D), BF),
+            jax.ShapeDtypeStruct((NY * REL * TILE, 16 * TILE), BF),
         ),
         in_specs=[IN_HBM] * 8,
-        out_specs=(ANY,) * 4,
+        out_specs=(ANY,) * 4 + (VM,),
         scratch_shapes=[
             pltpu.VMEM((4, NZ * NX, EB), jnp.int32),
             pltpu.VMEM((1, NZ * NX), jnp.int32),
@@ -279,8 +282,8 @@
     )(owner, source, target, relation, count, tiles, states, weights)
 
 
-def adjacency_kernel(meta, tiles, adj):
-    adj[...] = jnp.zeros_like(adj)
+def adjacency_kernel(meta, tiles, zeros, adj):
+    del zeros
 
     def slots(c, carry):
         for s in range(SLOTS):
@@ -297,28 +300,31 @@
     lax.fori_loop(0, NC, slots, 0)
 
 
-def adjacency(meta, tiles):
+def adjacency(meta, tiles, zeros):
     return pl.pallas_call(
         adjacency_kernel,
         out_shape=jax.ShapeDtypeStruct((NY * REL * TILE, 16 * TILE), BF),
-        in_specs=[SM, VM],
+        in_specs=[SM, VM, VM],
         out_specs=VM,
+        input_output_aliases={2: 0},
         compiler_params=params(6),
-    )(meta, tiles)
+    )(meta, tiles, zeros)
 
 
 def main_kernel(
     adj, xp, weights, states, cotangent,
-    layer_o, own_o, v_buf, wa, wb,
-    tq, tc_buf, ty_src, ty_buf, tg, m_own, m_src, m_buf, my_src, my_buf, slope_s, zs, gw,
-    xw_src, xw_buf, zw_src, zw_buf, aw_buf, wb_src, g_in, g_src, g_buf, gx_src, gx_buf,
-    bx_buf, b_src, b_buf, v_src,
+    layer_o, g_o, wa, wb,
+    tq, tc_buf, ty_src, ty_buf, tg, m_own, m_src, m_buf, my_src, my_buf, slope_s, zs,
+    gw_a, xw_src_a, xw_buf_a, zw_src_a, zw_buf_a, aw_buf_a,
+    gw_b, xw_src_b, xw_buf_b, zw_src_b, zw_buf_b, aw_buf_b, wb_src, g_in, g_src, g_buf, gx_src, gx_buf,
+    bx_buf, gb_src, gb_buf, v_src, v_buf,
     tc_s, tc_r, ty_s, ty_r, mc_s, mc_r, my_s, my_r, s_s, s_r, f_s, f_r,
-    xw_s, xw_r, zw_s, zw_r, aw_s, aw_r, wa_s, wa_r, wb_s, wb_r, g_s, g_r, gx_s, gx_r,
-    bx_s, bx_r, b_s, b_r, v_s, v_r,
+    xw_s, xw_r, zw_s, zw_r, aw_s, aw_r, wa_s, wa_r, wb_s, wb_r, g_s, g_r, gx_s, gx_r, bx_s, bx_r, gb_s, gb_r, v_s, v_r,
 ):
     over_rows = (((0,), (0,)), ((), ()))
     over_columns = (((1,), (1,)), ((), ()))
+    gw, xw_src, xw_buf = (gw_a, gw_b), (xw_src_a, xw_src_b), (xw_buf_a, xw_buf_b)
+    zw_src, zw_buf, aw_buf = (zw_src_a, zw_src_b), (zw_buf_a, zw_buf_b), (aw_buf_a, aw_buf_b)
     z, x, y, p = place()
     core = (z, x, y, 1 - p)
     shifts = (2, 1, 3)
@@ -350,15 +356,25 @@
 
     ty_copies = {}
 
-    def transforms_on(n):
+    def transforms_on(n, send_now=True):
         t = order[n]
         t_copies[n].wait_recv()
         for j, q in enumerate(ys):
             yi = q[2]
             ty_src[j, t] = (tq[p, t, yi].astype(F32) + tc_buf[t, yi].astype(F32)).astype(BF)
-            a = send(ty_src.at[j, t], ty_buf.at[j, t], ty_s.at[j, n], ty_r.at[j, n], *q)
+            if send_now:
+                a = send(ty_src.at[j, t], ty_buf.at[j, t], ty_s.at[j, n, 0], ty_r.at[j, n, 0], *q)
+                a.start()
+                ty_copies[j, n, 0] = a
+
+    def transforms_part(n, r):
+        t = order[n]
+        for j, q in enumerate(ys):
+            a = send(
+                ty_src.at[j, t, r], ty_buf.at[j, t, r], ty_s.at[j, n, r], ty_r.at[j, n, r], *q
+            )
             a.start()
-            ty_copies[j, n] = a
+            ty_copies[j, n, r] = a
 
     for n, t in enumerate(order):
         rows = pl.ds(pl.multiple_of(t * D, D), D)
@@ -403,9 +419,12 @@
         a.start()
         s_copies.append(a)
     for n in (2, 3):
-        transforms_on(n)
+        transforms_on(n, False)
+        transforms_part(n, 0)
+    for n in (2, 3):
+        transforms_part(n, 1)
     layer_o[...] = pre * sigma
-    own_o[...] = lax.dot_general(slope, w_self, over_columns, preferred_element_type=F32)
+    g_o[...] = lax.dot_general(slope, w_self, over_columns, preferred_element_type=F32)
     f_copies = []
     for i in (1, 2, 0):
         s_copies[i].wait_recv()
@@ -413,16 +432,21 @@
         a = send(ref, ref, f_s.at[i], f_r.at[i], *core)
         a.start()
         f_copies.append(a)
+    def transposed(core_of):
+        rows = jnp.concatenate([slope_s[t * 2 + core_of] for t in range(NY)], axis=0)
+        for r in range(REL):
+            part = lax.dot_general(rows, weights[r], over_columns, preferred_element_type=F32)
+            part = part.astype(BF)
+            for t in range(NY):
+                at = pl.multiple_of(t * D + r * TILE + core_of * ROWS, ROWS)
+                zs[pl.ds(at, ROWS), :] = part[t * ROWS : (t + 1) * ROWS]
+
+    transposed(p)
     s_copies[3].wait_recv()
     for a in f_copies:
         a.wait_recv()
-
+    transposed(1 - p)
     whole = slope_s[...].reshape(D, D)
-    for r in range(REL):
-        part = lax.dot_general(whole, weights[r], over_columns, preferred_element_type=F32)
-        part = part.astype(BF)
-        for t in range(NY):
-            zs[t * D + r * TILE : t * D + (r + 1) * TILE, :] = part[t * TILE : (t + 1) * TILE]
 
     def gradients(k):
         columns = pl.ds(pl.multiple_of(k * D, D), D)
@@ -436,17 +460,14 @@
     g_copies = {}
     hops = {(d, i): 4 if (i < 2) == (d == 0) else 3 for d in range(2) for i in range(NX)}
 
-    def toward(d, left):
-        return (z + left) % NZ if d == 0 else (z - left + NZ) % NZ
-
-    def chain(s):
+    def chain(s, only=(3, 4)):
         for i in range(NX):
             xi = (x + i) % NX
             for d, q in ((0, up), (1, down)):
                 left = hops[d, i] - s
-                if left <= 0:
+                if left <= 0 or hops[d, i] not in only:
                     continue
-                zd = toward(d, left)
+                zd = (z + left) % NZ if d == 0 else (z - left + NZ) % NZ
                 if s == 0:
                     src = g_in.at[zd, xi, pl.ds(0, HA)]
                 else:
@@ -460,9 +481,9 @@
                 g_copies[d, s, i] = a
 
     bx_copies = {}
-    b_copies = {}
-
-    def across(n, k):
+
+    def across(n):
+        k = near[n]
         two = pl.ds(2 * k, 2)
         for j, q in enumerate(xs):
             a = send(
@@ -475,98 +496,124 @@
         for j in range(3):
             bx_copies[j, n].wait_recv()
 
-    def x_sum(zd, h):
-        columns = slice(h * 256, (h + 1) * 256)
-        total = g_in[zd, x, HA:, columns].astype(F32)
+    gb_copies = {}
+
+    def x_sum(zd):
+        total = g_in[zd, x, HA:].astype(F32)
         for j in range(3):
-            total = total + bx_buf[j, zd, :, columns].astype(F32)
+            total = total + bx_buf[j, zd].astype(F32)
         return total
 
-    def second_chain(s):
-        for h in range(2):
-            for d, q in ((0, up), (1, down)):
-                left = (4 if h == d else 3) - s
-                if left <= 0:
-                    continue
-                total = x_sum(toward(d, left), h)
-                if s > 0:
-                    b_copies[d, s - 1, h].wait_recv()
-                    total = total + b_buf[d, s - 1, h].astype(F32)
-                b_src[d, s, h] = total.astype(BF)
-                a = send(b_src.at[d, s, h], b_buf.at[d, s, h], b_s.at[d, s, h], b_r.at[d, s, h], *q)
-                a.start()
-                b_copies[d, s, h] = a
+    def second(i):
+        zd = (z + i) % NZ
+        gb_src[i] = x_sum(zd).astype(BF)
+        a = send(gb_src.at[i], gb_buf.at[i], gb_s.at[i], gb_r.at[i], zd, x, y, p)
+        a.start()
+        gb_copies[i] = a
 
     pair = z // 2
     odd = 2 * (z % 2)
     near = ((pair + 2) % 4, (pair + 1 + odd) % 4, (pair + 3 + odd) % 4, pair)
-    for n in (0, 1):
-        gradients(near[n])
-        across(n, near[n])
-    chain(0)
+    columns = pl.ds(pl.multiple_of(y * TILE, TILE), TILE)
+    xw_copies, zw_copies, aw_copies, w_copies = [[], []], [[], []], [[], []], []
+
+    def weight_part(r):
+        for (j, n, q), a in ty_copies.items():
+            if q == r:
+                a.wait_recv()
+        for t in range(NY):
+            total = tq[p, t, y, r].astype(F32) + tc_buf[t, y, r].astype(F32)
+            for j in range(3):
+                total = total + ty_buf[j, t, r].astype(F32)
+            tg[r, t * TILE : (t + 1) * TILE, :] = total.astype(BF)
+        part = lax.dot_general(tg[r], whole, over_rows, preferred_element_type=F32)
+        rows_of = [half(part, True), half(part, False)]
+        if r == 1:
+            part = lax.dot_general(states[:, columns], whole, over_rows, preferred_element_type=F32)
+            rows_of.insert(1, half(part, True))
+        for m, v in enumerate(rows_of):
+            for q in range(NX):
+                gw[r][q, m * ROWS : (m + 1) * ROWS, :] = v[:, q * WC : (q + 1) * WC]
+        for i in range(3):
+            xw_src[r][i] = gw[r][xs[i][1]].astype(BF)
+            a = send(xw_src[r].at[i], xw_buf[r].at[i], xw_s.at[r, i], xw_r.at[r, i], *xs[i])
+            a.start()
+            xw_copies[r].append(a)
+
+    def weight_x(r):
+        total = gw[r][x]
+        for i, a in enumerate(xw_copies[r]):
+            a.wait_recv()
+            total = total + xw_buf[r][i].astype(F32)
+        total = total.reshape(NZ, PART[r] // NZ, WC)
+        if EIGHTH[r] > PART[r] // NZ:
+            padding = jnp.zeros((NZ, EIGHTH[r] - PART[r] // NZ, WC), F32)
+            total = jnp.concatenate([total, padding], axis=1)
+        zw_src[r][...] = total.astype(BF)
+        for i, q in enumerate(around):
+            a = send(zw_src[r].at[q[0]], zw_buf[r].at[i], zw_s.at[r, i], zw_r.at[r, i], *q)
+            a.start()
+            zw_copies[r].append(a)
+
+    def weight_z(r):
+        total = zw_src[r][z].astype(F32)
+        for i, a in enumerate(zw_copies[r]):
+            a.wait_recv()
+            total = total + zw_buf[r][i].astype(F32)
+        aw_buf[r][z] = total.astype(BF)
+        for i, q in enumerate(around):
+            a = send(aw_buf[r].at[z], aw_buf[r].at[z], aw_s.at[r, i], aw_r.at[r, i], *q)
+            a.start()
+            aw_copies[r].append(a)
+
+    def weight_out(r):
+        for a in aw_copies[r]:
+            a.wait_recv()
+        done = aw_buf[r][...].astype(F32)[:, : PART[r] // NZ].reshape(PART[r], WC).astype(BF)
+        mine, other = pl.ds(r * ROWS, (r + 1) * ROWS), pl.ds(r * ROWS, ROWS)
+        wa[x, mine, :] = done[: (r + 1) * ROWS]
+        wb_src[other, :] = done[(r + 1) * ROWS :]
+        for i, q in enumerate(xs):
+            ref = wa.at[x, mine]
+            w_copies.append(send(ref, ref, wa_s.at[r, i], wa_r.at[r, i], *q))
+        for i, q in enumerate(xo + [core]):
+            w_copies.append(
+                send(wb_src.at[other], wb.at[x, other], wb_s.at[r, i], wb_r.at[r, i], *q)
+            )
+        for a in w_copies[-7:]:
+            a.start()
+
+    gradients(near[0])
+    across(0)
+    chain(0, (4,))
+    gradients(near[1])
+    across(1)
+    chain(0, (3,))
+    weight_part(0)
     gradients(near[2])
-    across(2, near[2])
+    across(2)
     chain(1)
+    weight_part(1)
     gradients(near[3])
-    across(3, near[3])
+    across(3)
+    weight_x(0)
+    chain(2)
     across_wait(0)
     across_wait(1)
-    second_chain(0)
-
-    for a in ty_copies.values():
-        a.wait_recv()
-    for t in range(NY):
-        total = tq[p, t, y].astype(F32) + tc_buf[t, y].astype(F32)
-        for j in range(3):
-            total = total + ty_buf[j, t].astype(F32)
-        for r in range(2):
-            tg[r, t * TILE : (t + 1) * TILE, :] = total[r].astype(BF)
-    parts = [
-        lax.dot_general(tg[r], whole, over_rows, preferred_element_type=F32) for r in range(2)
-    ]
-    columns = pl.ds(pl.multiple_of(y * TILE, TILE), TILE)
-    self_part = lax.dot_general(states[:, columns], whole, over_rows, preferred_element_type=F32)
-    rows_of = [half(v, True) for v in parts] + [half(self_part, True)] + [half(v, False) for v in parts]
-    for m, v in enumerate(rows_of):
-        for q in range(NX):
-            gw[q, m * ROWS : (m + 1) * ROWS, :] = v[:, q * WC : (q + 1) * WC]
-    xw_copies = []
-    for i in range(3):
-        xw_src[i] = gw[xs[i][1]].astype(BF)
-        a = send(xw_src.at[i], xw_buf.at[i], xw_s.at[i], xw_r.at[i], *xs[i])
-        a.start()
-        xw_copies.append(a)
-    chain(2)
+    for i in (4, 3, 5):
+        second(i)
+    weight_z(0)
+    weight_x(1)
+    chain(3)
     across_wait(2)
-    second_chain(1)
-    total = gw[x]
-    for i, a in enumerate(xw_copies):
-        a.wait_recv()
-        total = total + xw_buf[i].astype(F32)
-    padding = jnp.zeros((NZ, ZROWS - WROWS // NZ, WC), F32)
-    zw_src[...] = jnp.concatenate(
-        [total.reshape(NZ, WROWS // NZ, WC), padding], axis=1
-    ).astype(BF)
-    zw_copies = []
-    for i, q in enumerate(around):
-        a = send(zw_src.at[q[0]], zw_buf.at[i], zw_s.at[i], zw_r.at[i], *q)
-        a.start()
-        zw_copies.append(a)
-    chain(3)
+    for i in (2, 6):
+        second(i)
+    weight_out(0)
+    weight_z(1)
     across_wait(3)
-    second_chain(2)
-    total = zw_src[z].astype(F32)
-    for i, a in enumerate(zw_copies):
-        a.wait_recv()
-        total = total + zw_buf[i].astype(F32)
-    aw_buf[z] = total.astype(BF)
-    aw_copies = []
-    for i, q in enumerate(around):
-        a = send(aw_buf.at[z], aw_buf.at[z], aw_s.at[i], aw_r.at[i], *q)
-        a.start()
-        aw_copies.append(a)
-
-    second_chain(3)
+    for i in (1, 7):
+        second(i)
+
     gx_copies = []
     own = None
     for i in (1, 2, 3, 0):
@@ -584,30 +631,16 @@
         else:
             own = part
 
-    for a in aw_copies:
+    weight_out(1)
+    total = x_sum(z)
+    for i, a in gb_copies.items():
         a.wait_recv()
-    done = aw_buf[...].astype(F32)[:, : WROWS // NZ].reshape(WROWS, WC).astype(BF)
-    wa[x] = done[: 3 * ROWS]
-    wb_src[...] = done[3 * ROWS :]
-    w_copies = []
-    for i, q in enumerate(xs):
-        w_copies.append(send(wa.at[x], wa.at[x], wa_s.at[i], wa_r.at[i], *q))
-    for i, q in enumerate(xo + [core]):
-        w_copies.append(send(wb_src, wb.at[x], wb_s.at[i], wb_r.at[i], *q))
-    for a in w_copies:
-        a.start()
-
+        total = total + gb_buf[i].astype(F32)
+    v_src[HA:] = total.astype(BF)
     for i, a in enumerate(gx_copies):
         a.wait_recv()
         own = own + gx_buf[i].astype(F32)
     v_src[:HA] = own.astype(BF)
-    for h in range(2):
-        part = x_sum(z, h)
-        for d in range(2):
-            last = (4 if h == d else 3) - 1
-            b_copies[d, last, h].wait_recv()
-            part = part + b_buf[d, last, h].astype(F32)
-        v_src[HA:, h * 256 : (h + 1) * 256] = part.astype(BF)
 
     @pl.when(jnp.logical_not(is_self))
     def _():
@@ -619,13 +652,15 @@
     def _():
         v_buf[...] = v_src[...]
 
+    g_o[...] = g_o[...] + v_buf[...].astype(F32)
     for a in w_copies:
         a.wait()
     for a in m_copies + t_copies + my_copies + s_copies + f_copies:
         a.wait_send()
-    for a in xw_copies + zw_copies + aw_copies + gx_copies:
-        a.wait_send()
-    for some in (ty_copies, g_copies, bx_copies, b_copies):
+    for copies in xw_copies + zw_copies + aw_copies + [gx_copies]:
+        for a in copies:
+            a.wait_send()
+    for some in (ty_copies, g_copies, bx_copies, gb_copies):
         for a in some.values():
             a.wait_send()
 
@@ -636,12 +671,11 @@
         out_shape=(
             jax.ShapeDtypeStruct((ROWS, D), F32),
             jax.ShapeDtypeStruct((ROWS, D), F32),
-            jax.ShapeDtypeStruct((ROWS, D), BF),
             jax.ShapeDtypeStruct((NX, 3 * ROWS, WC), BF),
             jax.ShapeDtypeStruct((NX, 2 * ROWS, WC), BF),
         ),
         in_specs=[VM] * 5,
-        out_specs=(VM,) * 5,
+        out_specs=(VM,) * 4,
         scratch_shapes=[
             pltpu.VMEM((2, NY, NY, 2, TILE, TILE), BF),
             pltpu.VMEM((NY, NY, 2, TILE, TILE), BF),
@@ -655,12 +689,18 @@
             pltpu.VMEM((3, ROWS, D), BF),
             pltpu.VMEM((NC, ROWS, D), BF),
             pltpu.VMEM((NY * D, D), BF),
-            pltpu.VMEM((NX, WROWS, WC), F32),
-            pltpu.VMEM((3, WROWS, WC), BF),
-            pltpu.VMEM((3, WROWS, WC), BF),
-            pltpu.VMEM((NZ, ZROWS, WC), BF),
-            pltpu.VMEM((7, ZROWS, WC), BF),
-            pltpu.VMEM((NZ, ZROWS, WC), BF),
+            *(
+                v
+                for r in range(2)
+                for v in (
+                    pltpu.VMEM((NX, PART[r], WC), F32),
+                    pltpu.VMEM((3, PART[r], WC), BF),
+                    pltpu.VMEM((3, PART[r], WC), BF),
+                    pltpu.VMEM((NZ, EIGHTH[r], WC), BF),
+                    pltpu.VMEM((7, EIGHTH[r], WC), BF),
+                    pltpu.VMEM((NZ, EIGHTH[r], WC), BF),
+                )
+            ),
             pltpu.VMEM((2 * ROWS, WC), BF),
             pltpu.VMEM((NZ, NX, ROWS, D), BF),
             pltpu.VMEM((2, 3, NX, HA, D), BF),
@@ -668,23 +708,24 @@
             pltpu.VMEM((3, HA, D), BF),
             pltpu.VMEM((3, HA, D), BF),
             pltpu.VMEM((3, NZ, HB, D), BF),
-            pltpu.VMEM((2, 4, 2, HB, 256), BF),
-            pltpu.VMEM((2, 4, 2, HB, 256), BF),
+            pltpu.VMEM((NZ, HB, D), BF),
+            pltpu.VMEM((NZ, HB, D), BF),
             pltpu.VMEM((ROWS, D), BF),
-            DMA((4,)), DMA((4,)), DMA((3, 4)), DMA((3, 4)), DMA((4,)), DMA((4,)), DMA((3,)), DMA((3,)),
+            pltpu.VMEM((ROWS, D), BF),
+            DMA((4,)), DMA((4,)), DMA((3, 4, 2)), DMA((3, 4, 2)), DMA((4,)), DMA((4,)), DMA((3,)), DMA((3,)),
             DMA((4,)), DMA((4,)), DMA((3,)), DMA((3,)),
-            DMA((3,)), DMA((3,)), DMA((7,)), DMA((7,)), DMA((7,)), DMA((7,)), DMA((3,)), DMA((3,)),
-            DMA((4,)), DMA((4,)), DMA((2, 4, 4)), DMA((2, 4, 4)), DMA((3,)), DMA((3,)),
-            DMA((3, 4)), DMA((3, 4)), DMA((2, 4, 2)), DMA((2, 4, 2)), DMA(()), DMA(()),
+            DMA((2, 3)), DMA((2, 3)), DMA((2, 7)), DMA((2, 7)), DMA((2, 7)), DMA((2, 7)),
+            DMA((2, 3)), DMA((2, 3)), DMA((2, 4)), DMA((2, 4)), DMA((2, 4, 4)), DMA((2, 4, 4)), DMA((3,)), DMA((3,)),
+            DMA((3, 4)), DMA((3, 4)), DMA((8,)), DMA((8,)), DMA(()), DMA(()),
         ],
         compiler_params=params(32, 1),
     )(adj, xp, weights, states, cotangent)
 
 
-def close_kernel(layer, own, v, wa, wb, layer_o, g_o, w_o):
+def close_kernel(layer, g, wa, wb, layer_o, g_o, w_o):
     p = lax.axis_index("replica")
     layer_o[...] = layer[...]
-    g_o[...] = own[...] + v[...].astype(F32)
+    g_o[...] = g[...]
     for q in range(NX):
         columns = slice(q * WC, (q + 1) * WC)
         for m in range(2):
@@ -695,7 +736,7 @@
         w_o[REL, :, columns] = wa[q, 2 * ROWS :, :].astype(F32)
 
 
-def close(layer, own, v, wa, wb):
+def close(layer, g, wa, wb):
     return pl.pallas_call(
         close_kernel,
         out_shape=(
@@ -703,10 +744,10 @@
             jax.ShapeDtypeStruct((ROWS, D), F32),
             jax.ShapeDtypeStruct((REL + 1, ROWS, D), F32),
         ),
-        in_specs=[VM] * 5,
+        in_specs=[VM] * 4,
         out_specs=(VM, VM, VM),
         compiler_params=params(8),
-    )(layer, own, v, wa, wb)
+    )(layer, g, wa, wb)
 
 
 def shards(
@@ -729,10 +770,10 @@
     tiles = edge_tiles.reshape(EB, TILE, TILE)
     given = (owner, source, target, relation, count, tiles, states, weights)
     given = (pltpu.with_memory_space_constraint(v, pltpu.HBM) for v in given)
-    tiles, meta, xp, full = deal(*given)
-    adj = adjacency(meta, tiles)
-    layer, own, v, wa, wb = main(adj, xp.reshape(-1, D), full, states, cotangent)
-    return close(layer, own, v, wa, wb)
+    tiles, meta, xp, full, zeros = deal(*given)
+    adj = adjacency(meta, tiles, zeros)
+    layer, g, wa, wb = main(adj, xp.reshape(-1, D), full, states, cotangent)
+    return close(layer, g, wa, wb)
 
 
 def solution(mesh):

time: 107 us -> 105 us (0.981)
  Pallas kernels: 106 us -> 104 us
    pallas_call x1, Pallas kernels: 62.8 us -> 61.7 us  [main(): pl.pallas_call(main_kernel, out_shape=(jax.ShapeDtypeStruct((ROWS, D), F3...]
where the time goes in v5:
time: 105 us
  Pallas kernels  104 us (99%)
    pallas_call x1, Pallas kernels, main(): pl.pallas_call(main_kernel, out_shape=(jax.ShapeDtypeStruct((ROWS, D), F3...  61.7 us
    pallas_call x1, Pallas kernels, deal(): pl.pallas_call(deal_kernel, out_shape=(jax.ShapeDtypeStruct((NC, SLOTS, T...  39.6 us
    pallas_call x1, Pallas kernels, adjacency(): pl.pallas_call(adjacency_kernel, out_shape=jax.ShapeDtypeStruct((NY * REL...  2.13 us

profile of v5, /device:TPU:24, one launch (start us, length us, event | category | flops | bytes accessed | tf_op | source)
XLA Modules:
  0.0 105.1 jit_solution(2843443036767638964)
XLA Ops:
  0.6 39.6 %shard_map.112 = (bf16[8,8,128,128]{3,2,1,0:T(8,128)(2,1)S(1)}, s32[8,8,128]{2,1,0:T(8,128)S(1)}, bf16[8,4,64,512]{3,2,1,0:T(8,128)(2,1)S(1)}, bf16[5,512,512]{2,1,0:T(8,128)(2,1)S(1)}, bf16[2048,2048]{1,0:T(8,128)(2,1)S(1)}) custom-call(s32[32,48]{1,0:T(8,128)} %bitcast.9, s32[32,48]{1,0:T(8,128)} %bitcast.10, s32[32,48]{1,0:T(8,128)} %bitcast.11, ...), custom_call_target="tpu_custom_call" | custom-call | tf_op jit(solution)/shard_map/pallas_call | solution.py:258
  40.2 0.0 copy-start
  40.2 0.0 copy-start.1
  40.3 2.1 %shard_map.113.adj = bf16[2048,2048]{1,0:T(8,128)(2,1)S(1)} custom-call(s32[8,8,128]{2,1,0:T(8,128)S(1)} %get-tuple-element.12.meta, bf16[8,8,128,128]{3,2,1,0:T(8,128)(2,1)S(1)} %get-tuple-element.13.tiles, bf16[2048,2048]{1,0:T(8,128)(2,1)S(1)} %get-tuple-element.14.zeros), custom_call_target="tpu_custom_call", output_to_operand_aliasing={{}: (2, {})} | custom-call | tf_op jit(solution)/shard_map/pallas_call | solution.py:304
  42.4 0.0 copy-done
  42.4 0.0 copy-done.1
  42.4 61.7 %shard_map.114 = (f32[64,512]{1,0:T(8,128)S(1)}, f32[64,512]{1,0:T(8,128)S(1)}, bf16[4,192,128]{2,1,0:T(8,128)(2,1)S(1)}, bf16[4,128,128]{2,1,0:T(8,128)(2,1)S(1)}) custom-call(bf16[2048,2048]{1,0:T(8,128)(2,1)S(1)} %shard_map.113.adj, bf16[2048,512]{1,0:T(8,128)(2,1)S(1)} %bitcast.7, bf16[5,512,512]{2,1,0:T(8,128)(2,1)S(1)} %get-tuple-element.16.weights, ...), custom_call_target="tpu_custom_call" | custom-call | tf_op jit(solution)/shard_map/pallas_call | solution.py:669
  104.1 1.0 shard_map.115
Async XLA Ops:
  40.2 2.2 %copy-start = (bf16[512,512]{1,0:T(8,128)(2,1)S(1)}, bf16[512,512]{1,0:T(8,128)(2,1)}, u32[]{:S(2)}) copy-start(bf16[512,512]{1,0:T(8,128)(2,1)} %states.3) | copy-start | bytes 1572868
  40.2 2.2 %copy-start.1 = (bf16[512,512]{1,0:T(8,128)(2,1)S(1)}, bf16[512,512]{1,0:T(8,128)(2,1)}, u32[]{:S(2)}) copy-start(bf16[512,512]{1,0:T(8,128)(2,1)} %cotangent.1) | copy-start | bytes 1572868

commit v6 on v5

--- a/solution.py
+++ b/solution.py
@@ -394,13 +394,10 @@
         m_copies.append(a)
         if n > 0:
             messages_on(n - 1)
-        if n == 1:
-            transforms_on(0)
         a = send(tq.at[1 - p, t], tc_buf.at[t], tc_s.at[n], tc_r.at[n], *core)
         a.start()
         t_copies.append(a)
 
-    transforms_on(1)
 
     w_self = weights[REL]
     pre = jnp.dot(states[share, :], w_self, preferred_element_type=F32)
@@ -418,10 +415,10 @@
         a = send(mine, mine, s_s.at[i], s_r.at[i], *q)
         a.start()
         s_copies.append(a)
-    for n in (2, 3):
+    for n in (0, 1, 2, 3):
         transforms_on(n, False)
         transforms_part(n, 0)
-    for n in (2, 3):
+    for n in (0, 1, 2, 3):
         transforms_part(n, 1)
     layer_o[...] = pre * sigma
     g_o[...] = lax.dot_general(slope, w_self, over_columns, preferred_element_type=F32)

time: 105 us -> 103 us (0.981)
    pallas_call x1, Pallas kernels: 61.7 us -> 59.9 us  [main(): pl.pallas_call(main_kernel, out_shape=(jax.ShapeDtypeStruct((ROWS, D), F3...]
where the time goes in v6:
time: 103 us
  Pallas kernels  103 us (100%)
    pallas_call x1, Pallas kernels, main(): pl.pallas_call(main_kernel, out_shape=(jax.ShapeDtypeStruct((ROWS, D), F3...  59.9 us
    pallas_call x1, Pallas kernels, deal(): pl.pallas_call(deal_kernel, out_shape=(jax.ShapeDtypeStruct((NC, SLOTS, T...  39.6 us

profile of v6, /device:TPU:24, one launch (start us, length us, event | category | flops | bytes accessed | tf_op | source)
XLA Modules:
  0.0 103.2 jit_solution(488777732702673431)
XLA Ops:
  0.6 39.6 %shard_map.112 = (bf16[8,8,128,128]{3,2,1,0:T(8,128)(2,1)S(1)}, s32[8,8,128]{2,1,0:T(8,128)S(1)}, bf16[8,4,64,512]{3,2,1,0:T(8,128)(2,1)S(1)}, bf16[5,512,512]{2,1,0:T(8,128)(2,1)S(1)}, bf16[2048,2048]{1,0:T(8,128)(2,1)S(1)}) custom-call(s32[32,48]{1,0:T(8,128)} %bitcast.9, s32[32,48]{1,0:T(8,128)} %bitcast.10, s32[32,48]{1,0:T(8,128)} %bitcast.11, ...), custom_call_target="tpu_custom_call" | custom-call | tf_op jit(solution)/shard_map/pallas_call | solution.py:258
  40.2 0.0 copy-start
  40.2 0.0 copy-start.1
  40.3 2.0 %shard_map.113.adj = bf16[2048,2048]{1,0:T(8,128)(2,1)S(1)} custom-call(s32[8,8,128]{2,1,0:T(8,128)S(1)} %get-tuple-element.12.meta, bf16[8,8,128,128]{3,2,1,0:T(8,128)(2,1)S(1)} %get-tuple-element.13.tiles, bf16[2048,2048]{1,0:T(8,128)(2,1)S(1)} %get-tuple-element.14.zeros), custom_call_target="tpu_custom_call", output_to_operand_aliasing={{}: (2, {})} | custom-call | tf_op jit(solution)/shard_map/pallas_call | solution.py:304
  42.3 0.0 copy-done
  42.3 0.0 copy-done.1
  42.3 59.9 %shard_map.114 = (f32[64,512]{1,0:T(8,128)S(1)}, f32[64,512]{1,0:T(8,128)S(1)}, bf16[4,192,128]{2,1,0:T(8,128)(2,1)S(1)}, bf16[4,128,128]{2,1,0:T(8,128)(2,1)S(1)}) custom-call(bf16[2048,2048]{1,0:T(8,128)(2,1)S(1)} %shard_map.113.adj, bf16[2048,512]{1,0:T(8,128)(2,1)S(1)} %bitcast.7, bf16[5,512,512]{2,1,0:T(8,128)(2,1)S(1)} %get-tuple-element.16.weights, ...), custom_call_target="tpu_custom_call" | custom-call | tf_op jit(solution)/shard_map/pallas_call | solution.py:666
  102.2 1.0 shard_map.115
Async XLA Ops:
  40.2 2.1 %copy-start = (bf16[512,512]{1,0:T(8,128)(2,1)S(1)}, bf16[512,512]{1,0:T(8,128)(2,1)}, u32[]{:S(2)}) copy-start(bf16[512,512]{1,0:T(8,128)(2,1)} %states.3) | copy-start | bytes 1572868
  40.2 2.1 %copy-start.1 = (bf16[512,512]{1,0:T(8,128)(2,1)S(1)}, bf16[512,512]{1,0:T(8,128)(2,1)}, u32[]{:S(2)}) copy-start(bf16[512,512]{1,0:T(8,128)(2,1)} %cotangent.1) | copy-start | bytes 1572868

commit v7 on v6

--- a/solution.py
+++ b/solution.py
@@ -113,13 +113,17 @@
     load_tiles.start()
     arrived = greet(peers + xs + [up, down], (target, is_self))
     c = y * 2 + p
-    piece = states.at[pl.ds(pl.multiple_of((p * NY + y) * ROWS, ROWS), ROWS)]
+    at = pl.multiple_of((p * NY + y) * ROWS, ROWS)
+    piece = states.at[pl.ds(at, ROWS)]
+    pieces = [states.at[pl.ds(pl.multiple_of(at + h * 32, 32), 32)] for h in range(2)]
 
     arrived()
 
     @pl.when(jnp.logical_not(is_self))
     def _():
-        send(piece, xp.at[target[0], target[1]], v_send, v_recv, *target).start()
+        for h in range(2):
+            dst = xp.at[target[0], target[1], pl.ds(h * 32, 32)]
+            send(pieces[h], dst, v_send.at[h], v_recv.at[h], *target).start()
 
     @pl.when(is_self)
     def _():
@@ -175,21 +179,26 @@
 
         lax.fori_loop(0, SLOTS, one, 0)
 
-    x_copies = [
-        send(xp.at[z, x], xp.at[z, x], x_send.at[i], x_recv.at[i], *q) for i, q in enumerate(xs)
-    ]
+    x_copies = {}
+    for h in range(2):
+        ref = xp.at[z, x, pl.ds(h * 32, 32)]
+        for i, q in enumerate(xs):
+            x_copies[h, i] = send(ref, ref, x_send.at[h, i], x_recv.at[h, i], *q)
 
     def x_phase():
-        @pl.when(jnp.logical_not(is_self))
-        def _():
-            send(piece, xp.at[z, x], v_send, v_recv, *target).wait()
-
         @pl.when(is_self)
         def _():
             pltpu.make_async_copy(piece, xp.at[z, x], own_sems.at[0]).wait()
 
-        for a in x_copies:
-            a.start()
+        for h in range(2):
+
+            @pl.when(jnp.logical_not(is_self))
+            def _():
+                dst = xp.at[z, x, pl.ds(h * 32, 32)]
+                send(pieces[h], dst, v_send.at[h], v_recv.at[h], *target).wait()
+
+            for i in range(3):
+                x_copies[h, i].start()
 
     tile_copies = []
     for i, q in enumerate(peers):
@@ -217,18 +226,19 @@
     wc_copies = []
     z_copies = {}
     for s in range(4):
-        for i in range(NX):
+        for i, h in ((i, h) for i in range(NX) for h in range(2)):
             xi = (x + i) % NX
             if s == 0 and i > 0:
-                x_copies[3 - i].wait_recv()
+                x_copies[h, 3 - i].wait_recv()
             for d, q in ((0, up), (1, down)):
-                if s > 0 and (d, s - 1, i) in z_copies:
-                    z_copies[d, s - 1, i].wait_recv()
+                if s > 0 and (d, s - 1, i, h) in z_copies:
+                    z_copies[d, s - 1, i, h].wait_recv()
                 if s < 3 or (i < 2) == (d == 0):
                     zs = (z - s + NZ) % NZ if d == 0 else (z + s) % NZ
-                    a = send(xp.at[zs, xi], xp.at[zs, xi], z_send.at[d, s, i], z_recv.at[d, s, i], *q)
+                    ref = xp.at[zs, xi, pl.ds(h * 32, 32)]
+                    a = send(ref, ref, z_send.at[d, s, i, h], z_recv.at[d, s, i, h], *q)
                     a.start()
-                    z_copies[d, s, i] = a
+                    z_copies[d, s, i, h] = a
         if s == 0:
             for i, yi in enumerate(((y + 3) % NY, (y + 1) % NY, (y + 2) % NY)):
                 wy_copies[i].wait_recv()
@@ -245,10 +255,10 @@
                 a = send(ref, ref, wc_send.at[i], wc_recv.at[i], *core)
                 a.start()
                 wc_copies.append(a)
-    for (d, s, i), a in z_copies.items():
+    for (d, s, i, h), a in z_copies.items():
         if s == 3:
             a.wait_recv()
-    for a in x_copies + list(z_copies.values()) + wy_copies + wx_copies:
+    for a in list(x_copies.values()) + list(z_copies.values()) + wy_copies + wx_copies:
         a.wait_send()
     for a in own_copies + wc_copies + tile_copies:
         a.wait()
@@ -274,8 +284,8 @@
             pltpu.SMEM((NC * 4, 128), jnp.int32),
             pltpu.VMEM((NC, 8, 128), jnp.int32),
             pltpu.VMEM((NC, SLOTS, TILE, TILE), BF),
-            DMA((7,)), DMA((4,)), DMA((7,)), DMA((7,)), DMA((7,)), DMA((7,)), DMA(()), DMA(()),
-            DMA((3,)), DMA((3,)), DMA((2, 4, 4)), DMA((2, 4, 4)),
+            DMA((7,)), DMA((4,)), DMA((7,)), DMA((7,)), DMA((7,)), DMA((7,)), DMA((2,)), DMA((2,)),
+            DMA((2, 3)), DMA((2, 3)), DMA((2, 4, 4, 2)), DMA((2, 4, 4, 2)),
             DMA((3,)), DMA((3,)), DMA((3, 3)), DMA((3, 3)), DMA((3,)), DMA((3,)),
         ],
         compiler_params=params(8, 0),

time: 103 us -> 103 us (level)
  no operation moved by 1% of the time
where the time goes in v7:
time: 103 us
  Pallas kernels  102 us (99%)
    pallas_call x1, Pallas kernels, main(): pl.pallas_call(main_kernel, out_shape=(jax.ShapeDtypeStruct((ROWS, D), F3...  59.8 us
    pallas_call x1, Pallas kernels, deal(): pl.pallas_call(deal_kernel, out_shape=(jax.ShapeDtypeStruct((NC, SLOTS, T...  39.4 us

profile of v7, /device:TPU:24, one launch (start us, length us, event | category | flops | bytes accessed | tf_op | source)
XLA Modules:
  0.0 102.9 jit_solution(7474121160460237737)
XLA Ops:
  0.6 39.4 %shard_map.112 = (bf16[8,8,128,128]{3,2,1,0:T(8,128)(2,1)S(1)}, s32[8,8,128]{2,1,0:T(8,128)S(1)}, bf16[8,4,64,512]{3,2,1,0:T(8,128)(2,1)S(1)}, bf16[5,512,512]{2,1,0:T(8,128)(2,1)S(1)}, bf16[2048,2048]{1,0:T(8,128)(2,1)S(1)}) custom-call(s32[32,48]{1,0:T(8,128)} %bitcast.9, s32[32,48]{1,0:T(8,128)} %bitcast.10, s32[32,48]{1,0:T(8,128)} %bitcast.11, ...), custom_call_target="tpu_custom_call" | custom-call | tf_op jit(solution)/shard_map/pallas_call | solution.py:268
  40.0 0.0 copy-start
  40.0 0.0 copy-start.1
  40.1 2.1 %shard_map.113.adj = bf16[2048,2048]{1,0:T(8,128)(2,1)S(1)} custom-call(s32[8,8,128]{2,1,0:T(8,128)S(1)} %get-tuple-element.12.meta, bf16[8,8,128,128]{3,2,1,0:T(8,128)(2,1)S(1)} %get-tuple-element.13.tiles, bf16[2048,2048]{1,0:T(8,128)(2,1)S(1)} %get-tuple-element.14.zeros), custom_call_target="tpu_custom_call", output_to_operand_aliasing={{}: (2, {})} | custom-call | tf_op jit(solution)/shard_map/pallas_call | solution.py:314
  42.1 0.0 copy-done
  42.1 0.0 copy-done.1
  42.1 59.8 %shard_map.114 = (f32[64,512]{1,0:T(8,128)S(1)}, f32[64,512]{1,0:T(8,128)S(1)}, bf16[4,192,128]{2,1,0:T(8,128)(2,1)S(1)}, bf16[4,128,128]{2,1,0:T(8,128)(2,1)S(1)}) custom-call(bf16[2048,2048]{1,0:T(8,128)(2,1)S(1)} %shard_map.113.adj, bf16[2048,512]{1,0:T(8,128)(2,1)S(1)} %bitcast.7, bf16[5,512,512]{2,1,0:T(8,128)(2,1)S(1)} %get-tuple-element.16.weights, ...), custom_call_target="tpu_custom_call" | custom-call | tf_op jit(solution)/shard_map/pallas_call | solution.py:676
  101.9 1.0 shard_map.115
Async XLA Ops:
  40.0 2.1 %copy-start = (bf16[512,512]{1,0:T(8,128)(2,1)S(1)}, bf16[512,512]{1,0:T(8,128)(2,1)}, u32[]{:S(2)}) copy-start(bf16[512,512]{1,0:T(8,128)(2,1)} %states.3) | copy-start | bytes 1572868
  40.0 2.1 %copy-start.1 = (bf16[512,512]{1,0:T(8,128)(2,1)S(1)}, bf16[512,512]{1,0:T(8,128)(2,1)}, u32[]{:S(2)}) copy-start(bf16[512,512]{1,0:T(8,128)(2,1)} %cotangent.1) | copy-start | bytes 1572868
